TPU v7x, 32 devices: a whole 2x2x4 slice. The times are simulated.
32 devices in a mesh: blk: 4 (over x, core), uly: 2 (over y), tp: 4 (over z).
Axes of the slice: x: 2, y: 2, z: 4, core: 2. Of those that a mesh axis runs over, the one named last changes fastest.
Arguments:
- hidden: bfloat16 [4096, 8192], P(('blk', 'uly')), may hold values from -8 to 8
- norm_gain: bfloat16 [8192], replicated, may hold values from 0.099609375 to 1.8984375
- query_key_value_weight: bfloat16 [8192, 4, 1280], P('uly', 'tp'), may hold values from -1 to 1
- w_out: bfloat16 [4096, 8192], P('tp', 'uly'), may hold values from -0.5 to 0.5
- doc_ids: int32 [4096], replicated, may hold values from 0 to 7, never falling along the last dimension, each value on 1 to 2048 neighbouring positions
- block_order: int32 [8], replicated, may hold values from 0 to 7, each once
Outputs:
- attn_out: bfloat16 [4096, 8192], P(('blk', 'tp'), 'uly')
Inputs may be any that keep to these rules, and one draw needn't show every extreme that they name: `doc_ids`: never falls along the sequence; every document holds 1 to 2048 positions and one holds exactly 2048. Array rows c * 512 to (c + 1) * 512 - 1 hold sequence block block_order[c]; every block appears once.
All inputs are finite; a program needn't handle non-finite values.
Results may differ from a plain program's by a relative error of at most 0.029.
Values may be sent and summed in bfloat16 or wider, within the bound.
No kernel may reach another device: no remote copies, remote signals or barrier semaphores. Data moves between devices by JAX's collectives and lax.ppermute only.
A program may use at most 128 MiB of HBM per device.

v0:
```python
import math

import jax
import jax.numpy as jnp
from jax import lax
from jax.sharding import PartitionSpec as P

QUERY_HEAD_COUNT = 32
KV_HEAD_COUNT = 4
HEAD_SIZE = 128
BLOCK = 512


THETA = 500000.0
NEG_BIG = -1e30


def rope_tables(positions):
    half_dim = HEAD_SIZE // 2
    lane_ids = jnp.arange(half_dim).astype(jnp.float32)
    base_freq = jnp.power(THETA, -2.0 * lane_ids / HEAD_SIZE)
    wavelen = 2.0 * math.pi / base_freq
    smooth = (8192.0 / wavelen - 1.0) / 3.0
    blended = (1.0 - smooth) * base_freq / 8.0 + smooth * base_freq
    scaled = jnp.where(
        wavelen > 8192.0, base_freq / 8.0, jnp.where(wavelen < 2048.0, base_freq, blended)
    )
    angles = positions.astype(jnp.float32)[:, None] * scaled[None, :]
    return (jnp.cos(angles), jnp.sin(angles))


def rotate(values, cos_table, sin_table):
    half_dim = values.shape[-1] // 2
    leading = values[..., :half_dim]
    trailing = values[..., half_dim:]
    cos_part = cos_table[:, None, :]
    sin_part = sin_table[:, None, :]
    return jnp.concatenate(
        [leading * cos_part - trailing * sin_part, trailing * cos_part + leading * sin_part],
        axis=-1,
    )


def positions_of(block_order, row_ids):
    block_ids = row_ids // BLOCK
    matches = block_ids[:, None] == jnp.arange(block_order.shape[0])[None, :]
    seq_block = jnp.sum(jnp.where(matches, block_order[None, :], 0), axis=1)
    return seq_block * BLOCK + row_ids % BLOCK


def make_attend(queries, query_pos, query_seg, doc_ids, block_order):
    head_dim = queries.shape[2]
    inv_root = 1.0 / math.sqrt(head_dim)

    def attend(running, pieces, offset):
        key_piece, value_piece = pieces
        key_count = key_piece.shape[0]
        block_size = key_count
        while block_size > 1024 and block_size % 2 == 0:
            block_size = block_size // 2
        block_total = key_count // block_size
        piece_pos = positions_of(block_order, jnp.arange(key_count))
        piece_seg = jnp.take(doc_ids, piece_pos)
        stacked = (
            key_piece.reshape(block_total, block_size, head_dim),
            value_piece.reshape(block_total, block_size, head_dim),
            piece_pos.reshape(block_total, block_size),
            piece_seg.reshape(block_total, block_size),
        )

        def one_block(softmax_state, block_data):
            key_blk, value_blk, pos_blk, seg_blk = block_data
            allowed = (pos_blk[None, :] <= query_pos[:, None]) & (
                seg_blk[None, :] == query_seg[:, None]
            )
            row_max, row_sum, weighted = softmax_state
            scores = (
                jnp.einsum("qhd,kd->hqk", queries, key_blk, preferred_element_type=jnp.float32)
                * inv_root
            )
            scores = jnp.where(allowed[None, :, :], scores, NEG_BIG)
            new_max = jnp.maximum(row_max, jnp.max(scores, axis=2))
            weights = jnp.where(allowed[None, :, :], jnp.exp(scores - new_max[:, :, None]), 0.0)
            factor = jnp.exp(row_max - new_max)
            new_sum = row_sum * factor + jnp.sum(weights, axis=2)
            product = jnp.einsum(
                "hqk,kd->hqd",
                weights.astype(jnp.bfloat16),
                value_blk,
                preferred_element_type=jnp.float32,
            )
            next_state = (new_max, new_sum, weighted * factor[:, :, None] + product)
            return (next_state, None)

        final_state, unused = lax.scan(one_block, running, stacked)
        return final_state

    return attend


def on_device(hidden, norm_gain, query_key_value_weight, w_out, doc_ids, block_order):
    group_width = QUERY_HEAD_COUNT // KV_HEAD_COUNT
    heads_here = group_width // lax.axis_size("uly")
    widened = hidden.astype(jnp.float32)
    inverse_rms = lax.rsqrt(jnp.mean(widened * widened, axis=1, keepdims=True) + 1e-05)
    rms_scaled = (widened * inverse_rms * norm_gain.astype(jnp.float32)[None, :]).astype(
        jnp.bfloat16
    )
    regrouped = lax.all_to_all(rms_scaled, "uly", split_axis=1, concat_axis=0, tiled=True)
    block_len = regrouped.shape[0]
    local_weights = query_key_value_weight.reshape(
        query_key_value_weight.shape[0], (group_width + 2) * HEAD_SIZE
    )
    partial_proj = jnp.dot(regrouped, local_weights, preferred_element_type=jnp.float32)
    query_part = partial_proj[:, : group_width * HEAD_SIZE]
    pair_part = partial_proj[:, group_width * HEAD_SIZE :]
    first_row = lax.axis_index("blk") * block_len
    query_pos = positions_of(block_order, first_row + jnp.arange(block_len))
    query_seg = jnp.take(doc_ids, query_pos)
    cos_query, sin_query = rope_tables(query_pos)
    query_sum, pair_sum = (
        lax.psum_scatter(query_part, "uly", scatter_dimension=1, tiled=True),
        lax.psum_scatter(pair_part, "uly", scatter_dimension=0, tiled=True),
    )
    key_len = pair_sum.shape[0]
    key_start = first_row + lax.axis_index("uly") * key_len
    key_pos = positions_of(block_order, key_start + jnp.arange(key_len))
    cos_key, sin_key = rope_tables(key_pos)
    queries = rotate(
        query_sum.reshape(block_len, heads_here, HEAD_SIZE), cos_query, sin_query
    ).astype(jnp.bfloat16)
    keys_local = rotate(pair_sum[:, None, :HEAD_SIZE], cos_key, sin_key)[:, 0, :].astype(
        jnp.bfloat16
    )
    values_local = pair_sum[:, HEAD_SIZE:].astype(jnp.bfloat16)
    attend = make_attend(queries, query_pos, query_seg, doc_ids, block_order)
    initial = (
        jnp.full((heads_here, block_len), NEG_BIG, jnp.float32),
        jnp.zeros((heads_here, block_len), jnp.float32),
        jnp.zeros((heads_here, block_len, HEAD_SIZE), jnp.float32),
    )
    final_state = attend(
        initial,
        (
            lax.all_gather(keys_local, ("blk", "uly"), axis=0, tiled=True),
            lax.all_gather(values_local, ("blk", "uly"), axis=0, tiled=True),
        ),
        jnp.int32(0),
    )
    row_max, row_sum, weighted = final_state
    attended = (weighted / row_sum[:, :, None]).astype(jnp.bfloat16)
    head_weights = w_out.reshape(group_width, HEAD_SIZE, w_out.shape[1])
    projected_rows = jnp.einsum(
        "hqd,hdn->qn",
        lax.all_gather(attended, "uly", axis=0, tiled=True),
        head_weights,
        preferred_element_type=jnp.float32,
    )
    return lax.psum_scatter(
        projected_rows.astype(jnp.bfloat16), "tp", scatter_dimension=0, tiled=True
    )


def solution(mesh):
    return jax.shard_map(
        on_device,
        mesh=mesh,
        in_specs=(P(("blk", "uly"), None), P(), P("uly", "tp", None), P("tp", "uly"), P(), P()),
        out_specs=P(("blk", "tp"), "uly"),
        check_vma=False,
    )
```

profile of v0, /device:TPU:0, one launch (start us, length us, event | category | flops | bytes accessed | tf_op | source)
XLA Modules:
  0.0 596.5 jit_solution(17927666600049915901)
XLA Ops:
  6.5 12.0 %copy.29 = bf16[512,8192]{0,1:T(8,128)(2,1)} copy(bf16[512,8192]{1,0:T(8,128)(2,1)} %param.8) | data formatting | bytes 16777216 | tf_op args[0]
  18.6 5.3 fusion.20
  26.5 98.1 %all_to_all.19 = bf16[512,2,4096]{0,2,1:T(8,128)(2,1)} all-to-all(bf16[512,2,4096]{0,2,1:T(8,128)(2,1)S(1)} %bitcast.62), channel_id=1, replica_groups=mesh['blk'=4,'uly'=2,'tp'=4] {'uly'}, dimensions={1} | all-to-all | bytes 16777216 | tf_op jit(solution)/shard_map/all_to_all | solution.py:109
  124.6 11.8 %copy.30 = bf16[2,512,4096]{2,1,0:T(8,128)(2,1)} copy(bf16[2,512,4096]{1,2,0:T(8,128)(2,1)} %bitcast.63) | data formatting | bytes 16777216 | tf_op jit(solution)/shard_map/all_to_all | solution.py:109
  136.4 15.1 %fusion.23 = f32[1024,1280]{1,0:T(8,128)S(1)} fusion(bf16[1024,4096]{1,0:T(8,128)(2,1)} %bitcast.64, bf16[4096,1,1280]{2,0,1:T(8,128)(2,1)} %param.10), kind=kOutput, calls=%fused_computation.34 | convolution fusion | flops 10737418240 | bytes 24117248 | tf_op jit(solution)/shard_map/dot_general | solution.py:114
  155.4 20.7 %reduce-scatter.4.cloned.1.call-done = f32[512,256]{0,1:T(8,128)} async-done(((f32[1024,256]{0,1:T(8,128)}), f32[512,256]{0,1:T(8,128)}) %reduce-scatter.4.cloned.1.call-update) | async-done | bytes 524304 | tf_op jit(solution)/shard_map/reduce_scatter | solution.py:123
  180.1 4.8 slice.41
  185.5 6.2 %gather_fusion.1 = s32[1024]{0:T(1024)S(1)} fusion(s32[4096]{0:T(1024)S(1)} %copy-done, s32[1024]{0:T(1024)S(1)} %broadcast_clamp_fusion.1), kind=kCustom, calls=%fused_computation.1 | custom fusion | bytes 12288 | tf_op jit(solution)/shard_map/jit(_take)/gather | solution.py:119
  191.8 23.0 %gather_fusion = s32[4096]{0:T(1024)S(1)} fusion(s32[4096]{0:T(1024)S(1)} %copy-done, s32[4096]{0:T(1024)S(1)} %broadcast_clamp_fusion), kind=kCustom, calls=%fused_computation | custom fusion | bytes 49152 | tf_op jit(solution)/shard_map/jit(_take)/gather | solution.py:63
  214.9 3.1 multiply_cosine_fusion
  219.6 8.2 %all-gather.5.cloned.1.call-done = bf16[4096,128]{0,1:T(8,128)(2,1)} async-done(((bf16[512,128]{0,1:T(8,128)(2,1)}), bf16[4096,128]{0,1:T(8,128)(2,1)}) %all-gather.5.cloned.1.call-update) | async-done | bytes 1048592 | tf_op jit(solution)/shard_map/all_gather | solution.py:146
  230.0 54.4 %reduce-scatter.6.cloned.1.call-done = f32[1024,512]{1,0:T(8,128)} async-done(((f32[1024,1024]{1,0:T(8,128)}), f32[1024,512]{1,0:T(8,128)}) %reduce-scatter.6.cloned.1.call-update) | async-done | bytes 2097168 | tf_op jit(solution)/shard_map/reduce_scatter | solution.py:122
  288.7 107.2 %while.15 = (s32[]{:T(128)}, f32[4,1024]{1,0:T(4,128)S(1)}, f32[4,1024]{1,0:T(4,128)S(1)}, f32[4,1024,128]{2,1,0:T(8,128)}, s32[4,1024]{1,0:T(4,128)S(1)}, /*ind...) while((s32[]{:T(128)}, f32[4,1024]{1,0:T(4,128)S(1)}, ...), condition=%wide.region_9.10_spmd.clone, body=%wide.region_6.9_spmd.clone.sunk | while | flops 2206748672 | bytes 127697576 | solution.py:95
  289.9 7.3 %fusion.70 = (f32[4,1024]{1,0:T(4,128)S(1)}, f32[1024,1024,4]{1,0,2:T(8,128)}) fusion(pred[1024,1024]{0,1:T(8,128)(4,1)S(1)} %compare_and_fusion.2, bf16[1024,4,128]{2,0,1:T(8,128)(2,1)S(1)} %get-tuple-element.267, bf16[4,1024,128]{2,1,0:T(8,128)(2,1)S(1)} %get-tuple-element.266, s32[]{:T(128)} %get-tuple-element.245), kind=kOutput, calls=%fused_computation.4.clone.1 | convolution fusion | flops 1086320640 | bytes 19152900 | tf_op jit(solution)/shard_map/while/body/eval_jaxpr/qhd,kd->hqk/dot_general | solution.py:78
  297.3 8.2 %fusion.71 = f32[4,1024]{1,0:T(4,128)S(1)} fusion(f32[1024,1024,4]{1,0,2:T(8,128)} %get-tuple-element.229, f32[4,1024]{1,0:T(4,128)S(1)} %select_maximum_fusion.2, pred[1024,1024]{0,1:T(8,128)(4,1)S(1)} %compare_and_fusion.2), kind=kLoop, calls=%fused_computation.6.clone.1 | loop fusion | flops 20967424 | bytes 17858560 | tf_op jit(solution)/shard_map/while/body/eval_jaxpr/reduce_sum | solution.py:85
  305.6 2.4 copy-done.2
  308.0 7.4 %fusion.73 = f32[4,1024,128]{2,1,0:T(8,128)} fusion(f32[4,1024,128]{2,1,0:T(8,128)} %get-tuple-element.248, f32[1024,1024,4]{1,0,2:T(8,128)S(1)} %copy-done.2, f32[4,1024]{1,0:T(4,128)S(1)} %select_maximum_fusion.2, pred[1024,1024]{0,1:T(8,128)(4,1)S(1)} %compare_and_fusion.2, f32[4,1024]{1,0:T(4,128)S(1)} %get-tuple-element.231, pred[]{:T(512)S(6)} %compare.37, ...), kind=kOutput, calls=%fused_computation.11.clone.1 | convolution fusion | flops 1096286208 | bytes 22315520 | tf_op jit(solution)/shard_map/while/body/eval_jaxpr/hqk,kd->hqd/dot_general | solution.py:86
  316.6 7.3 %fusion.70 = (f32[4,1024]{1,0:T(4,128)S(1)}, f32[1024,1024,4]{1,0,2:T(8,128)}) fusion(pred[1024,1024]{0,1:T(8,128)(4,1)S(1)} %compare_and_fusion.2, bf16[1024,4,128]{2,0,1:T(8,128)(2,1)S(1)} %get-tuple-element.267, bf16[4,1024,128]{2,1,0:T(8,128)(2,1)S(1)} %get-tuple-element.266, s32[]{:T(128)} %get-tuple-element.245), kind=kOutput, calls=%fused_computation.4.clone.1 | convolution fusion | flops 1086320640 | bytes 19152900 | tf_op jit(solution)/shard_map/while/body/eval_jaxpr/qhd,kd->hqk/dot_general | solution.py:78
  324.0 8.2 %fusion.71 = f32[4,1024]{1,0:T(4,128)S(1)} fusion(f32[1024,1024,4]{1,0,2:T(8,128)} %get-tuple-element.229, f32[4,1024]{1,0:T(4,128)S(1)} %select_maximum_fusion.2, pred[1024,1024]{0,1:T(8,128)(4,1)S(1)} %compare_and_fusion.2), kind=kLoop, calls=%fused_computation.6.clone.1 | loop fusion | flops 20967424 | bytes 17858560 | tf_op jit(solution)/shard_map/while/body/eval_jaxpr/reduce_sum | solution.py:85
  332.2 2.4 copy-done.2
  334.7 7.6 %fusion.73 = f32[4,1024,128]{2,1,0:T(8,128)} fusion(f32[4,1024,128]{2,1,0:T(8,128)} %get-tuple-element.248, f32[1024,1024,4]{1,0,2:T(8,128)S(1)} %copy-done.2, f32[4,1024]{1,0:T(4,128)S(1)} %select_maximum_fusion.2, pred[1024,1024]{0,1:T(8,128)(4,1)S(1)} %compare_and_fusion.2, f32[4,1024]{1,0:T(4,128)S(1)} %get-tuple-element.231, pred[]{:T(512)S(6)} %compare.37, ...), kind=kOutput, calls=%fused_computation.11.clone.1 | convolution fusion | flops 1096286208 | bytes 22315520 | tf_op jit(solution)/shard_map/while/body/eval_jaxpr/hqk,kd->hqd/dot_general | solution.py:86
  343.5 7.3 %fusion.70 = (f32[4,1024]{1,0:T(4,128)S(1)}, f32[1024,1024,4]{1,0,2:T(8,128)}) fusion(pred[1024,1024]{0,1:T(8,128)(4,1)S(1)} %compare_and_fusion.2, bf16[1024,4,128]{2,0,1:T(8,128)(2,1)S(1)} %get-tuple-element.267, bf16[4,1024,128]{2,1,0:T(8,128)(2,1)S(1)} %get-tuple-element.266, s32[]{:T(128)} %get-tuple-element.245), kind=kOutput, calls=%fused_computation.4.clone.1 | convolution fusion | flops 1086320640 | bytes 19152900 | tf_op jit(solution)/shard_map/while/body/eval_jaxpr/qhd,kd->hqk/dot_general | solution.py:78
  350.8 8.2 %fusion.71 = f32[4,1024]{1,0:T(4,128)S(1)} fusion(f32[1024,1024,4]{1,0,2:T(8,128)} %get-tuple-element.229, f32[4,1024]{1,0:T(4,128)S(1)} %select_maximum_fusion.2, pred[1024,1024]{0,1:T(8,128)(4,1)S(1)} %compare_and_fusion.2), kind=kLoop, calls=%fused_computation.6.clone.1 | loop fusion | flops 20967424 | bytes 17858560 | tf_op jit(solution)/shard_map/while/body/eval_jaxpr/reduce_sum | solution.py:85
  359.1 2.4 copy-done.2
  361.5 7.6 %fusion.73 = f32[4,1024,128]{2,1,0:T(8,128)} fusion(f32[4,1024,128]{2,1,0:T(8,128)} %get-tuple-element.248, f32[1024,1024,4]{1,0,2:T(8,128)S(1)} %copy-done.2, f32[4,1024]{1,0:T(4,128)S(1)} %select_maximum_fusion.2, pred[1024,1024]{0,1:T(8,128)(4,1)S(1)} %compare_and_fusion.2, f32[4,1024]{1,0:T(4,128)S(1)} %get-tuple-element.231, pred[]{:T(512)S(6)} %compare.37, ...), kind=kOutput, calls=%fused_computation.11.clone.1 | convolution fusion | flops 1096286208 | bytes 22315520 | tf_op jit(solution)/shard_map/while/body/eval_jaxpr/hqk,kd->hqd/dot_general | solution.py:86
  370.3 7.3 %fusion.70 = (f32[4,1024]{1,0:T(4,128)S(1)}, f32[1024,1024,4]{1,0,2:T(8,128)}) fusion(pred[1024,1024]{0,1:T(8,128)(4,1)S(1)} %compare_and_fusion.2, bf16[1024,4,128]{2,0,1:T(8,128)(2,1)S(1)} %get-tuple-element.267, bf16[4,1024,128]{2,1,0:T(8,128)(2,1)S(1)} %get-tuple-element.266, s32[]{:T(128)} %get-tuple-element.245), kind=kOutput, calls=%fused_computation.4.clone.1 | convolution fusion | flops 1086320640 | bytes 19152900 | tf_op jit(solution)/shard_map/while/body/eval_jaxpr/qhd,kd->hqk/dot_general | solution.py:78
  377.7 8.2 %fusion.71 = f32[4,1024]{1,0:T(4,128)S(1)} fusion(f32[1024,1024,4]{1,0,2:T(8,128)} %get-tuple-element.229, f32[4,1024]{1,0:T(4,128)S(1)} %select_maximum_fusion.2, pred[1024,1024]{0,1:T(8,128)(4,1)S(1)} %compare_and_fusion.2), kind=kLoop, calls=%fused_computation.6.clone.1 | loop fusion | flops 20967424 | bytes 17858560 | tf_op jit(solution)/shard_map/while/body/eval_jaxpr/reduce_sum | solution.py:85
  388.3 7.6 %fusion.73 = f32[4,1024,128]{2,1,0:T(8,128)} fusion(f32[4,1024,128]{2,1,0:T(8,128)} %get-tuple-element.248, f32[1024,1024,4]{1,0,2:T(8,128)S(1)} %copy-done.2, f32[4,1024]{1,0:T(4,128)S(1)} %select_maximum_fusion.2, pred[1024,1024]{0,1:T(8,128)(4,1)S(1)} %compare_and_fusion.2, f32[4,1024]{1,0:T(4,128)S(1)} %get-tuple-element.231, pred[]{:T(512)S(6)} %compare.37, ...), kind=kOutput, calls=%fused_computation.11.clone.1 | convolution fusion | flops 1096286208 | bytes 22315520 | tf_op jit(solution)/shard_map/while/body/eval_jaxpr/hqk,kd->hqd/dot_general | solution.py:86
  395.9 2.7 divide_convert_fusion
  398.7 33.2 %all-gather.7.cloned.1.call-done = bf16[8,1024,128]{2,1,0:T(8,128)(2,1)} async-done(((bf16[4,1024,128]{2,1,0:T(8,128)(2,1)}), bf16[8,1024,128]{2,1,0:T(8,128)(2,1)}) %all-gather.7.cloned.1.call-update) | async-done | bytes 2097168 | tf_op jit(solution)/shard_map/all_gather | solution.py:155
  432.0 13.0 %bitcast_convert_fusion = bf16[1024,4096]{1,0:T(8,128)(2,1)} fusion(bf16[8,1024,128]{2,1,0:T(8,128)(2,1)} %all-gather.7.cloned.1.call-done, bf16[8,128,4096]{2,1,0:T(8,128)(2,1)} %bitcast.73), kind=kOutput, calls=%fused_computation.33 | convolution fusion | flops 8594128896 | bytes 18874368 | tf_op jit(solution)/shard_map/hqd,hdn->qn/dot_general | solution.py:153
  445.0 144.6 %reduce-scatter.8.cloned.1.call-done = bf16[256,4096]{1,0:T(8,128)(2,1)} async-done(((bf16[1024,4096]{1,0:T(8,128)(2,1)}), bf16[256,4096]{1,0:T(8,128)(2,1)}) %reduce-scatter.8.cloned.1.call-update) | async-done | bytes 2097168 | tf_op jit(solution)/shard_map/reduce_scatter | solution.py:159
  (90 shorter events, 26.6 us)
Async XLA Ops:
  6.5 179.0 %copy-start = (s32[4096]{0:T(1024)S(1)}, s32[4096]{0:T(1024)}, u32[]{:S(2)}) copy-start(s32[4096]{0:T(1024)} %param.12) | copy-start | bytes 49156
  6.5 169.6 %reduce-scatter.4.cloned.1.call-start = ((), (), s32[]{:S(2)}) async-start(), calls=%async_computation.4 | async-start | bytes 1572864 | tf_op jit(solution)/shard_map/reduce_scatter | solution.py:123
  6.5 17.3 %copy-start.7 = (bf16[8192]{0:T(1024)(128)(2,1)S(1)}, bf16[8192]{0:T(1024)(128)(2,1)}, u32[]{:S(2)}) copy-start(bf16[8192]{0:T(1024)(128)(2,1)} %param.9) | copy-start | bytes 49156
  18.6 5.8 copy-start.3
  136.4 18.9 %copy-start.8 = (s32[8]{0:T(128)S(1)}, s32[8]{0:T(128)}, u32[]{:S(2)}) copy-start(s32[8]{0:T(128)} %param.13) | copy-start | bytes 100
  151.5 2.3 copy-start.4
  155.2 62.7 %all-gather.9.cloned.1.call-start = ((), (), s32[]{:S(2)}) async-start(), calls=%async_computation.9 | async-start | bytes 1179648 | tf_op jit(solution)/shard_map/all_gather | solution.py:145
  178.4 49.4 %all-gather.5.cloned.1.call-start = ((), (), s32[]{:S(2)}) async-start(), calls=%async_computation.6 | async-start | bytes 1179648 | tf_op jit(solution)/shard_map/all_gather | solution.py:146
  180.1 104.3 %reduce-scatter.6.cloned.1.call-start = ((), (), s32[]{:S(2)}) async-start(), calls=%async_computation.5 | async-start | bytes 6291456 | tf_op jit(solution)/shard_map/reduce_scatter | solution.py:122
  185.0 247.0 %all-gather.7.cloned.1.call-start = ((), (), s32[]{:S(2)}) async-start(), calls=%async_computation.7 | async-start | bytes 3145728 | tf_op jit(solution)/shard_map/all_gather | solution.py:155
  286.3 1.2 copy-start.5
  286.3 1.2 copy-start.6
  297.3 10.7 %copy-start.2 = (f32[1024,1024,4]{1,0,2:T(8,128)S(1)}, f32[1024,1024,4]{1,0,2:T(8,128)}, u32[]{:S(2)}) copy-start(f32[1024,1024,4]{1,0,2:T(8,128)} %get-tuple-element.229) | copy-start | bytes 50331652 | tf_op jit(solution)/shard_map/while
  324.0 10.7 %copy-start.2 = (f32[1024,1024,4]{1,0,2:T(8,128)S(1)}, f32[1024,1024,4]{1,0,2:T(8,128)}, u32[]{:S(2)}) copy-start(f32[1024,1024,4]{1,0,2:T(8,128)} %get-tuple-element.229) | copy-start | bytes 50331652 | tf_op jit(solution)/shard_map/while
  350.8 10.7 %copy-start.2 = (f32[1024,1024,4]{1,0,2:T(8,128)S(1)}, f32[1024,1024,4]{1,0,2:T(8,128)}, u32[]{:S(2)}) copy-start(f32[1024,1024,4]{1,0,2:T(8,128)} %get-tuple-element.229) | copy-start | bytes 50331652 | tf_op jit(solution)/shard_map/while
  377.6 10.7 %copy-start.2 = (f32[1024,1024,4]{1,0,2:T(8,128)S(1)}, f32[1024,1024,4]{1,0,2:T(8,128)}, u32[]{:S(2)}) copy-start(f32[1024,1024,4]{1,0,2:T(8,128)} %get-tuple-element.229) | copy-start | bytes 50331652 | tf_op jit(solution)/shard_map/while
  398.7 190.9 %reduce-scatter.8.cloned.1.call-start = ((), (), s32[]{:S(2)}) async-start(), calls=%async_computation.8 | async-start | bytes 10485760 | tf_op jit(solution)/shard_map/reduce_scatter | solution.py:159
  432.0 157.7 %copy-start.1 = (s32[4096]{0:T(1024)S(1)}, s32[4096]{0:T(1024)}, u32[]{:S(2)}) copy-start(s32[4096]{0:T(1024)} %param.12) | copy-start | bytes 49156
Sparse Core Ops, SparseCore 0:
  155.3 20.7 reduce-scatter.3
  178.5 23.5 all-gather.8
  204.2 23.5 all-gather.4
  230.0 54.3 reduce-scatter.5
  398.8 33.1 all-gather.6
  445.1 144.4 reduce-scatter.7
where the time goes:
time: 598 us; the launch traced here: 596 us
  waiting for transfers between devices  261 us (44%)
  blocking collectives  98.1 us (16%)
  matrix products  87.6 us (15%)
  local copies, waits for them, and re-layouts  81.2 us (14%)
  other arithmetic  53.9 us (9%)
  between operations  13.8 us (2%)
    reduce_scatter x1, waiting for transfers between devices, on_device(): lax.psum_scatter(projected_rows.astype(jnp.bfloat16), 'tp', scatter_dimen...  145 us
    all_to_all x1, blocking collectives, on_device(): lax.all_to_all(rms_scaled, 'uly', split_axis=1, concat_axis=0, tiled=True)  98.1 us
    reduce_scatter x1, waiting for transfers between devices, on_device(): lax.psum_scatter(query_part, 'uly', scatter_dimension=1, tiled=True)  54.4 us
    all_gather x1, waiting for transfers between devices, on_device(): lax.all_gather(attended, 'uly', axis=0, tiled=True)  33.2 us
    reduce_sum x4, other arithmetic, one_block(): new_sum = row_sum * factor + jnp.sum(weights, axis=2)  32.9 us
    dot_general x4, matrix products, one_block(): jnp.einsum('hqk,kd->hqd', weights.astype(jnp.bfloat16), value_blk, prefer...  30.2 us
    dot_general x4, matrix products, one_block(): jnp.einsum('qhd,kd->hqk', queries, key_blk, preferred_element_type=jnp.fl...  29.4 us
    gather x2, local copies, waits for them, and re-layouts, attend(): piece_seg = jnp.take(doc_ids, piece_pos)  23 us
  transfers between devices with their start and end apart: 6, of which 5 were waited for; matrix products, arithmetic and copies ran while one was open for 7% of the time, Pallas kernels for 0%

commit v1 on v0

--- a/solution.py
+++ b/solution.py
@@ -1,18 +1,22 @@
+import functools
 import math
 
 import jax
 import jax.numpy as jnp
 from jax import lax
+from jax.experimental import pallas as pl
+from jax.experimental.pallas import tpu as pltpu
 from jax.sharding import PartitionSpec as P
 
 QUERY_HEAD_COUNT = 32
 KV_HEAD_COUNT = 4
 HEAD_SIZE = 128
 BLOCK = 512
-
+GROUP_WIDTH = QUERY_HEAD_COUNT // KV_HEAD_COUNT
 
 THETA = 500000.0
 NEG_BIG = -1e30
+VMEM_LIMIT = 56 * 1024 * 1024
 
 
 def rope_tables(positions):
@@ -29,6 +33,259 @@
     return (jnp.cos(angles), jnp.sin(angles))
 
 
+def params(steps=1):
+    return pltpu.CompilerParams(
+        dimension_semantics=("arbitrary",) * steps, vmem_limit_bytes=VMEM_LIMIT
+    )
+
+
+def norm_kernel(hidden_ref, gain_ref, out_ref):
+    widened = hidden_ref[...].astype(jnp.float32)
+    inverse_rms = lax.rsqrt(jnp.mean(widened * widened, axis=1, keepdims=True) + 1e-05)
+    out_ref[...] = (widened * inverse_rms * gain_ref[...].astype(jnp.float32)).astype(jnp.bfloat16)
+
+
+def norm_rows(hidden, gain):
+    rows, width = hidden.shape
+    tile = 64
+    return pl.pallas_call(
+        norm_kernel,
+        grid=(rows // tile,),
+        in_specs=[
+            pl.BlockSpec((tile, width), lambda i: (i, 0)),
+            pl.BlockSpec((1, width), lambda i: (0, 0)),
+        ],
+        out_specs=pl.BlockSpec((tile, width), lambda i: (i, 0)),
+        out_shape=jax.ShapeDtypeStruct((rows, width), jnp.bfloat16),
+        compiler_params=params(),
+        cost_estimate=pl.CostEstimate(
+            flops=rows * width * 4, bytes_accessed=rows * width * 4, transcendentals=rows
+        ),
+    )(hidden, gain.reshape(1, width))
+
+
+def proj_kernel(rotated, order_ref, normed_ref, own_ref, q0, q1, q2, q3, cos_ref, sin_ref, out_ref, acc):
+    step = pl.program_id(0)
+
+    @pl.when(step == 0)
+    def _():
+        acc[...] = jnp.zeros_like(acc)
+
+    @pl.when(step < 4)
+    def _():
+        acc[...] += jnp.dot(normed_ref[...], own_ref[...], preferred_element_type=jnp.float32)
+
+    for i, quarter in enumerate((q0, q1, q2, q3)):
+
+        @pl.when(step == 4 + i)
+        def _(quarter=quarter):
+            acc[...] += jnp.dot(normed_ref[...], quarter[...], preferred_element_type=jnp.float32)
+
+    @pl.when(step == 7)
+    def _():
+        for i in range(out_ref.shape[1] // HEAD_SIZE):
+            lanes = slice(i * HEAD_SIZE, (i + 1) * HEAD_SIZE)
+            head = acc[:, lanes]
+            if i < rotated:
+                head = head * cos_ref[...] + pltpu.roll(head, HEAD_SIZE // 2, 1) * sin_ref[...]
+            out_ref[:, lanes] = head.astype(jnp.bfloat16)
+
+
+def project(order, normed, own, quarters, column_block, rotated, cos_table, sin_table):
+    rows, width = normed.shape
+    depth, columns = quarters[0].shape
+    whole = lambda k, s: (0, 0)
+    return pl.pallas_call(
+        functools.partial(proj_kernel, rotated),
+        grid_spec=pltpu.PrefetchScalarGridSpec(
+            num_scalar_prefetch=1,
+            grid=(8,),
+            in_specs=[
+                pl.BlockSpec((rows, depth), lambda k, s: (0, s[k])),
+                pl.BlockSpec((depth, columns), lambda k, s: (jnp.minimum(k, 3), column_block)),
+                *[pl.BlockSpec((depth, columns), whole) for _ in quarters],
+                pl.BlockSpec((rows, HEAD_SIZE), whole),
+                pl.BlockSpec((rows, HEAD_SIZE), whole),
+            ],
+            out_specs=pl.BlockSpec((rows, columns), whole),
+            scratch_shapes=[pltpu.VMEM((rows, columns), jnp.float32)],
+        ),
+        out_shape=jax.ShapeDtypeStruct((rows, columns), jnp.bfloat16),
+        compiler_params=params(),
+        cost_estimate=pl.CostEstimate(
+            flops=2 * rows * width * columns,
+            bytes_accessed=2 * (rows * width + width * columns),
+            transcendentals=0,
+        ),
+    )(order, normed, own, *quarters, cos_table, sin_table)
+
+
+def attend_kernel(info_ref, q_ref, kv_ref, qseg_ref, kseg_ref, out_ref, m_ref, l_ref, acc_ref):
+    my_block = info_ref[0]
+    first_block = info_ref[1]
+    scale = math.log2(math.e) / math.sqrt(HEAD_SIZE)
+    rows = q_ref.shape[0]
+    heads = q_ref.shape[1] // HEAD_SIZE
+
+    def one_block(block, diagonal):
+        slot = info_ref[2 + block]
+        keys = kv_ref[pl.ds(pl.multiple_of(slot * BLOCK, BLOCK), BLOCK), :HEAD_SIZE]
+        values = kv_ref[pl.ds(pl.multiple_of(slot * BLOCK, BLOCK), BLOCK), HEAD_SIZE:]
+        allowed = kseg_ref[block] == qseg_ref[...]
+        if diagonal:
+            allowed &= lax.broadcasted_iota(jnp.int32, (rows, BLOCK), 1) <= lax.broadcasted_iota(
+                jnp.int32, (rows, BLOCK), 0
+            )
+        for h in range(heads):
+            lanes = slice(h * HEAD_SIZE, (h + 1) * HEAD_SIZE)
+            scores = lax.dot_general(
+                q_ref[:, lanes], keys, (((1,), (1,)), ((), ())), preferred_element_type=jnp.float32
+            )
+            scores = jnp.where(allowed, scores, NEG_BIG)
+            block_max = jnp.max(scores, axis=1, keepdims=True)
+            if diagonal:
+                new_max = block_max
+            else:
+                old_max = m_ref[h]
+                new_max = jnp.maximum(old_max, block_max)
+            weights = jnp.exp2((scores - new_max) * scale)
+            block_sum = jnp.sum(weights, axis=1, keepdims=True)
+            product = jnp.dot(
+                weights.astype(jnp.bfloat16), values, preferred_element_type=jnp.float32
+            )
+            if diagonal:
+                l_ref[h] = block_sum
+                acc_ref[h] = product
+            else:
+                factor = jnp.exp2((old_max - new_max) * scale)
+                l_ref[h] = l_ref[h] * factor + block_sum
+                acc_ref[h] = acc_ref[h] * factor + product
+            m_ref[h] = new_max
+
+    one_block(my_block, True)
+
+    def body(i, carry):
+        one_block(my_block - i, False)
+        return carry
+
+    lax.fori_loop(1, my_block - first_block + 1, body, 0)
+    for h in range(heads):
+        out_ref[:, h * HEAD_SIZE : (h + 1) * HEAD_SIZE] = (acc_ref[h] / l_ref[h]).astype(
+            jnp.bfloat16
+        )
+
+
+def attend(info, queries, pairs, query_seg, key_seg):
+    rows, columns = queries.shape
+    heads = columns // HEAD_SIZE
+    return pl.pallas_call(
+        attend_kernel,
+        grid_spec=pltpu.PrefetchScalarGridSpec(
+            num_scalar_prefetch=1,
+            grid=(1,),
+            in_specs=[
+                pl.BlockSpec(queries.shape, lambda i, s: (0, 0)),
+                pl.BlockSpec(pairs.shape, lambda i, s: (0, 0)),
+                pl.BlockSpec(query_seg.shape, lambda i, s: (0, 0)),
+                pl.BlockSpec(key_seg.shape, lambda i, s: (0, 0, 0)),
+            ],
+            out_specs=pl.BlockSpec(queries.shape, lambda i, s: (0, 0)),
+            scratch_shapes=[
+                pltpu.VMEM((heads, rows, 1), jnp.float32),
+                pltpu.VMEM((heads, rows, 1), jnp.float32),
+                pltpu.VMEM((heads, rows, HEAD_SIZE), jnp.float32),
+            ],
+        ),
+        out_shape=jax.ShapeDtypeStruct(queries.shape, jnp.bfloat16),
+        compiler_params=params(),
+        cost_estimate=pl.CostEstimate(
+            flops=4 * rows * 4 * BLOCK * columns,
+            bytes_accessed=4 * pairs.size,
+            transcendentals=heads * rows * 4 * BLOCK,
+        ),
+    )(info, queries, pairs, query_seg, key_seg)
+
+
+def swap_uly(array):
+    return lax.ppermute(array, "uly", [(0, 1), (1, 0)])
+
+
+def swap_blk(array, bit):
+    return lax.ppermute(array, "blk", [(i, i ^ bit) for i in range(4)])
+
+
+def pick(table, index):
+    ids = jnp.arange(table.shape[0])
+    return jnp.sum(jnp.where(index[..., None] == ids, table, 0), axis=-1)
+
+
+def quarters_of(sent):
+    first = swap_uly(sent)
+    second = swap_blk(first, 2)
+    return (first, second, swap_blk(first, 1), swap_blk(second, 1))
+
+
+def one_block_each(hidden, norm_gain, query_key_value_weight, w_out, doc_ids, block_order):
+    blk, uly, tp = (lax.axis_index(name) for name in ("blk", "uly", "tp"))
+    weights = query_key_value_weight.reshape(query_key_value_weight.shape[0], -1)
+    depth = weights.shape[0] // 4
+    chunk = 2 * HEAD_SIZE
+    nblocks = block_order.shape[0]
+
+    column_blocks = [GROUP_WIDTH // 2, *range(GROUP_WIDTH // 2)]
+    received = []
+    for block in column_blocks:
+        sent = lax.dynamic_slice(weights, (blk * depth, block * chunk), (depth, chunk))
+        received.append(quarters_of(sent))
+
+    normed = norm_rows(hidden, norm_gain)
+
+    my_row = blk * 2 + uly
+    my_block = pick(block_order, my_row)
+    positions = my_block * BLOCK + jnp.arange(BLOCK)
+    cosine, sine = rope_tables(positions)
+    cos_table = jnp.concatenate([cosine, cosine], axis=1)
+    sin_table = jnp.concatenate([-sine, sine], axis=1)
+    own = uly * 4 + jnp.arange(4)
+    other = (1 - uly) * 4 + (blk ^ jnp.array([0, 2, 1, 3]))
+    order = jnp.concatenate([own, other]).astype(jnp.int32)
+
+    rows_of_slots = jnp.stack(
+        [(blk ^ c ^ x) * 2 + (uly ^ u) for c in (0, 1) for u in (0, 1) for x in (0, 2)]
+    )
+    blocks_of_slots = pick(block_order, rows_of_slots)
+    slots = jnp.arange(nblocks)
+    slot_of_block = jnp.sum(
+        jnp.where(blocks_of_slots[None, :] == slots[:, None], slots[None, :], 0), axis=1
+    )
+    query_seg = lax.dynamic_slice(doc_ids, (my_block * BLOCK,), (BLOCK,))
+    first_key = jnp.sum((doc_ids < query_seg[0]).astype(jnp.int32))
+    info = jnp.concatenate(
+        [jnp.stack([my_block, first_key // BLOCK]), slot_of_block]
+    ).astype(jnp.int32)
+    query_seg = query_seg[:, None]
+    key_seg = doc_ids.reshape(nblocks, 1, BLOCK)
+
+    pair = project(order, normed, weights, received[0], column_blocks[0], 1, cos_table, sin_table)
+    pair_y = swap_uly(pair)
+    pair_x = swap_blk(pair, 2)
+    pair_xy = swap_uly(pair_x)
+    near = jnp.concatenate([pair, pair_x, pair_y, pair_xy], axis=0)
+    pairs = jnp.concatenate([near, swap_blk(near, 1)], axis=0)
+
+    attended = []
+    for block, quarters in zip(column_blocks[1:], received[1:]):
+        queries = project(order, normed, weights, quarters, block, 2, cos_table, sin_table)
+        attended.append(attend(info, queries, pairs, query_seg, key_seg))
+
+    both = [jnp.where(uly == 0, jnp.stack([a, b]), jnp.stack([b, a])) for a, b in ((a, swap_uly(a)) for a in attended)]
+    gathered = jnp.concatenate([part.reshape(2 * BLOCK, chunk) for part in both], axis=1)
+    projected_rows = jnp.dot(gathered, w_out, preferred_element_type=jnp.float32)
+    return lax.psum_scatter(
+        projected_rows.astype(jnp.bfloat16), "tp", scatter_dimension=0, tiled=True
+    )
+
+
 def rotate(values, cos_table, sin_table):
     half_dim = values.shape[-1] // 2
     leading = values[..., :half_dim]
@@ -52,7 +309,7 @@
     head_dim = queries.shape[2]
     inv_root = 1.0 / math.sqrt(head_dim)
 
-    def attend(running, pieces, offset):
+    def attend_pieces(running, pieces):
         key_piece, value_piece = pieces
         key_count = key_piece.shape[0]
         block_size = key_count
@@ -95,11 +352,11 @@
         final_state, unused = lax.scan(one_block, running, stacked)
         return final_state
 
-    return attend
+    return attend_pieces
 
 
 def on_device(hidden, norm_gain, query_key_value_weight, w_out, doc_ids, block_order):
-    group_width = QUERY_HEAD_COUNT // KV_HEAD_COUNT
+    group_width = GROUP_WIDTH
     heads_here = group_width // lax.axis_size("uly")
     widened = hidden.astype(jnp.float32)
     inverse_rms = lax.rsqrt(jnp.mean(widened * widened, axis=1, keepdims=True) + 1e-05)
@@ -133,21 +390,19 @@
         jnp.bfloat16
     )
     values_local = pair_sum[:, HEAD_SIZE:].astype(jnp.bfloat16)
-    attend = make_attend(queries, query_pos, query_seg, doc_ids, block_order)
+    attend_pieces = make_attend(queries, query_pos, query_seg, doc_ids, block_order)
     initial = (
         jnp.full((heads_here, block_len), NEG_BIG, jnp.float32),
         jnp.zeros((heads_here, block_len), jnp.float32),
         jnp.zeros((heads_here, block_len, HEAD_SIZE), jnp.float32),
     )
-    final_state = attend(
+    row_max, row_sum, weighted = attend_pieces(
         initial,
         (
             lax.all_gather(keys_local, ("blk", "uly"), axis=0, tiled=True),
             lax.all_gather(values_local, ("blk", "uly"), axis=0, tiled=True),
         ),
-        jnp.int32(0),
-    )
-    row_max, row_sum, weighted = final_state
+    )
     attended = (weighted / row_sum[:, :, None]).astype(jnp.bfloat16)
     head_weights = w_out.reshape(group_width, HEAD_SIZE, w_out.shape[1])
     projected_rows = jnp.einsum(
@@ -162,10 +417,17 @@
 
 
 def solution(mesh):
-    return jax.shard_map(
-        on_device,
-        mesh=mesh,
-        in_specs=(P(("blk", "uly"), None), P(), P("uly", "tp", None), P("tp", "uly"), P(), P()),
-        out_specs=P(("blk", "tp"), "uly"),
-        check_vma=False,
-    )
+    sizes = dict(mesh.shape)
+
+    def whole(hidden, *rest):
+        tokens = hidden.shape[0]
+        fits = (sizes["blk"], sizes["uly"], sizes["tp"]) == (4, 2, 4) and tokens == 8 * BLOCK
+        return jax.shard_map(
+            one_block_each if fits else on_device,
+            mesh=mesh,
+            in_specs=(P(("blk", "uly"), None), P(), P("uly", "tp", None), P("tp", "uly"), P(), P()),
+            out_specs=P(("blk", "tp"), "uly"),
+            check_vma=False,
+        )(hidden, *rest)
+
+    return whole

time: 598 us -> 369 us (0.62)
  blocking collectives: 98.1 us -> 0 us
  Pallas kernels: 0 us -> 89.1 us
  matrix products: 87.6 us -> 14.3 us
  local copies, waits for them, and re-layouts: 81.2 us -> 12.4 us
  waiting for transfers between devices: 261 us -> 205 us
  other arithmetic: 53.9 us -> 6.41 us
  starting transfers between devices: 0.39 us -> 18.5 us
    all_to_all x1 -> x0, blocking collectives: 98.1 us -> none  [on_device(): lax.all_to_all(rms_scaled, 'uly', split_axis=1, concat_axis=0, tiled=True)]
    pallas_call x0 -> x10, Pallas kernels: none -> 89.1 us  [the longest x5 50.7 us: project(): pl.pallas_call(functools.partial(proj_kernel, rotated), grid_spec=pltpu.P...]
    dot_general x10 -> x1, matrix products: 87.6 us -> 14.3 us  [one_block_each(): jnp.dot(gathered, w_out, preferred_element_type=jnp.float32)]
    reduce_scatter x3 -> x1, waiting for transfers between devices: 220 us -> 160 us  [one_block_each(): lax.psum_scatter(projected_rows.astype(jnp.bfloat16), 'tp', scatter_dimen...]
    ppermute x0 -> x28, waiting for transfers between devices: none -> 45.7 us  [the longest x11 34.4 us: swap_uly(): return lax.ppermute(array, 'uly', [(0, 1), (1, 0)])]
    all_gather x3 -> x0, waiting for transfers between devices: 41.4 us -> none  [the longest x1 33.2 us: on_device(): lax.all_gather(attended, 'uly', axis=0, tiled=True)]
    reduce_sum x8 -> x4, other arithmetic: 38.5 us -> 2.22 us  [the longest x1 1.29 us: one_block_each(): first_key = jnp.sum((doc_ids < query_seg[0]).astype(jnp.int32))]
    gather x3 -> x0, local copies, waits for them, and re-layouts: 29.2 us -> none  [the longest x2 23 us: attend(): piece_seg = jnp.take(doc_ids, piece_pos)]
  transfers between devices with their start and end apart: 6 -> 29, of which waited for: 5 -> 7; matrix products, arithmetic and copies ran while one was open for 7% -> 3% of each run, Pallas kernels for 0% -> 23%
where the time goes in v1:
time: 369 us; the launch traced here: 363 us
  waiting for transfers between devices  205 us (56%)
  Pallas kernels  89.1 us (24%)
  starting transfers between devices  18.5 us (5%)
  between operations  16.5 us (4%)
  matrix products  14.3 us (4%)
  local copies, waits for them, and re-layouts  12.4 us (3%)
  other arithmetic  6.41 us (2%)
    reduce_scatter x1, waiting for transfers between devices, one_block_each(): lax.psum_scatter(projected_rows.astype(jnp.bfloat16), 'tp', scatter_dimen...  160 us
    pallas_call x5, Pallas kernels, project(): pl.pallas_call(functools.partial(proj_kernel, rotated), grid_spec=pltpu.P...  50.7 us
    ppermute x11, waiting for transfers between devices, swap_uly(): return lax.ppermute(array, 'uly', [(0, 1), (1, 0)])  34.4 us
    pallas_call x4, Pallas kernels, attend(): pl.pallas_call(attend_kernel, grid_spec=pltpu.PrefetchScalarGridSpec(num_...  27.7 us
    dot_general x1, matrix products, one_block_each(): jnp.dot(gathered, w_out, preferred_element_type=jnp.float32)  14.3 us
    ppermute x17, waiting for transfers between devices, swap_blk(): return lax.ppermute(array, 'blk', [(i, i ^ bit) for i in range(4)])  11.2 us
    ppermute x17, starting transfers between devices, swap_blk(): return lax.ppermute(array, 'blk', [(i, i ^ bit) for i in range(4)])  10.7 us
    pallas_call x1, Pallas kernels, norm_rows(): pl.pallas_call(norm_kernel, grid=(rows // tile,), in_specs=[pl.BlockSpec(...  10.6 us
  transfers between devices with their start and end apart: 29, of which 7 were waited for; matrix products, arithmetic and copies ran while one was open for 3% of the time, Pallas kernels for 23%

profile of v1, /device:TPU:0, one launch (start us, length us, event | category | flops | bytes accessed | tf_op | source)
XLA Modules:
  0.0 362.7 jit_solution(17918019412314855616)
XLA Ops:
  6.5 2.9 dynamic-slice_bitcast_fusion.4
  9.5 3.0 collective-permute-start.4
  12.5 12.8 %collective-permute-done.4.q0 = bf16[1024,256]{1,0:T(8,128)(2,1)} collective-permute-done((bf16[1024,256]{1,0:T(8,128)(2,1)S(1)}, bf16[1024,256]{1,0:T(8,128)(2,1)}, u32[]{:S(2)}, u32[]{:S(2)}) %collective-permute-start.4) | collective-permute-done | bytes 524320 | tf_op jit(solution)/shard_map/ppermute | solution.py:210
  25.3 2.0 collective-permute-start.5
  27.3 1.5 collective-permute-start.18
  30.6 5.9 %collective-permute-done.23.q0 = bf16[1024,256]{1,0:T(8,128)(2,1)S(1)} collective-permute-done((bf16[1024,256]{1,0:T(8,128)(2,1)S(1)}, bf16[1024,256]{1,0:T(8,128)(2,1)S(1)}, u32[]{:S(2)}, u32[]{:S(2)}) %collective-permute-start.23) | collective-permute-done | bytes 524320 | tf_op jit(solution)/shard_map/ppermute | solution.py:210
  36.4 2.0 collective-permute-start.24
  39.1 1.0 fusion.7
  40.1 7.6 %collective-permute-done.18.q0 = bf16[1024,256]{1,0:T(8,128)(2,1)S(1)} collective-permute-done((bf16[1024,256]{1,0:T(8,128)(2,1)S(1)}, bf16[1024,256]{1,0:T(8,128)(2,1)S(1)}, u32[]{:S(2)}, u32[]{:S(2)}) %collective-permute-start.18) | collective-permute-done | bytes 524320 | tf_op jit(solution)/shard_map/ppermute | solution.py:210
  47.7 2.1 collective-permute-start
  51.1 10.6 %shard_map.73.normed_ref = bf16[512,8192]{1,0:T(8,128)(2,1)} custom-call(bf16[512,8192]{1,0:T(8,128)(2,1)} %hidden_ref.1, bf16[1,8192]{1,0:T(2,128)(2,1)} %reshape.64.gain_ref), custom_call_target="tpu_custom_call" | custom-call | flops 16777216 | bytes 16777216 | tf_op jit(solution)/shard_map/pallas_call | solution.py:51
  61.8 1.6 collective-permute-start.19
  63.9 1.0 pad_maximum_fusion.1
  65.4 10.1 %shard_map.75 = bf16[512,256]{1,0:T(8,128)(2,1)} custom-call(s32[8]{0:T(128)} %pad_add_fusion.1.order_ref, bf16[512,8192]{1,0:T(8,128)(2,1)} %shard_map.73.normed_ref, bf16[4096,1280]{1,0:T(8,128)(2,1)} %bitcast.37, bf16[1024,256]{1,0:T(8,128)(2,1)} %collective-permute-done.4.q0, bf16[1024,256]{1,0:T(8,128)(2,1)} %collective-permute-done.5.q1, ...), custom_call_target="tpu_custom_call" | custom-call | flops 2147483648 | bytes 12582912 | tf_op jit(solution)/shard_map/pallas_call | solution.py:98
  76.2 1.3 convert_reduce_fusion
  79.7 0.9 copy.12.qseg_ref
  80.7 1.6 collective-permute-start.14
  83.4 1.6 collective-permute-done.8
  85.5 1.2 pad_add_fusion.info_ref
  86.8 10.3 %shard_map.81.q_ref = bf16[512,256]{1,0:T(8,128)(2,1)} custom-call(s32[8]{0:T(128)} %pad_add_fusion.1.order_ref, bf16[512,8192]{1,0:T(8,128)(2,1)} %shard_map.73.normed_ref, bf16[4096,1280]{1,0:T(8,128)(2,1)} %bitcast.38, bf16[1024,256]{1,0:T(8,128)(2,1)} %copy-done.3, bf16[1024,256]{1,0:T(8,128)(2,1)} %copy-done.5, ...), custom_call_target="tpu_custom_call" | custom-call | flops 2147483648 | bytes 12582912 | tf_op jit(solution)/shard_map/pallas_call | solution.py:98
  97.1 9.6 %collective-permute-done.1.q1 = bf16[1024,256]{1,0:T(8,128)(2,1)S(1)} collective-permute-done((bf16[1024,256]{1,0:T(8,128)(2,1)S(1)}, bf16[1024,256]{1,0:T(8,128)(2,1)S(1)}, u32[]{:S(2)}, u32[]{:S(2)}) %collective-permute-start.1) | collective-permute-done | bytes 524320 | tf_op jit(solution)/shard_map/ppermute | solution.py:214
  108.6 10.1 %shard_map.79.q_ref = bf16[512,256]{1,0:T(8,128)(2,1)} custom-call(s32[8]{0:T(128)} %pad_add_fusion.1.order_ref, bf16[512,8192]{1,0:T(8,128)(2,1)} %shard_map.73.normed_ref, bf16[4096,1280]{1,0:T(8,128)(2,1)} %bitcast.39, bf16[1024,256]{1,0:T(8,128)(2,1)} %copy-done.2, bf16[1024,256]{1,0:T(8,128)(2,1)} %collective-permute-done.19.q1, ...), custom_call_target="tpu_custom_call" | custom-call | flops 2147483648 | bytes 12582912 | tf_op jit(solution)/shard_map/pallas_call | solution.py:98
  120.3 10.1 %shard_map.77.q_ref = bf16[512,256]{1,0:T(8,128)(2,1)} custom-call(s32[8]{0:T(128)} %pad_add_fusion.1.order_ref, bf16[512,8192]{1,0:T(8,128)(2,1)} %shard_map.73.normed_ref, bf16[4096,1280]{1,0:T(8,128)(2,1)} %bitcast.40, bf16[1024,256]{1,0:T(8,128)(2,1)} %copy-done.1, bf16[1024,256]{1,0:T(8,128)(2,1)} %copy-done.8, bf16[1024,256]{1,0:T(8,128)(2,1)} %copy-done.11, ...), custom_call_target="tpu_custom_call" | custom-call | flops 2147483648 | bytes 12582912 | tf_op jit(solution)/shard_map/pallas_call | solution.py:98
  132.1 10.1 %shard_map.74.q_ref = bf16[512,256]{1,0:T(8,128)(2,1)} custom-call(s32[8]{0:T(128)} %pad_add_fusion.1.order_ref, bf16[512,8192]{1,0:T(8,128)(2,1)} %shard_map.73.normed_ref, bf16[4096,1280]{1,0:T(8,128)(2,1)} %bitcast.41, bf16[1024,256]{1,0:T(8,128)(2,1)} %copy-done.4, bf16[1024,256]{1,0:T(8,128)(2,1)} %copy-done.7, bf16[1024,256]{1,0:T(8,128)(2,1)} %copy-done.10, ...), custom_call_target="tpu_custom_call" | custom-call | flops 2147483648 | bytes 12582912 | tf_op jit(solution)/shard_map/pallas_call | solution.py:98
  144.4 1.0 constant_dynamic-update-slice_fusion.kv_ref
  145.4 6.8 %shard_map.82 = bf16[512,256]{1,0:T(8,128)(2,1)} custom-call(s32[10]{0:T(128)} %pad_add_fusion.info_ref, bf16[512,256]{1,0:T(8,128)(2,1)} %shard_map.81.q_ref, bf16[4096,256]{1,0:T(8,128)(2,1)} %constant_dynamic-update-slice_fusion.kv_ref, s32[512,1]{1,0:T(8,128)} %copy.12.qseg_ref, s32[8,1,512]{2,1,0:T(1,128)} %bitcast.54), custom_call_target="tpu_custom_call" | custom-call | flops 1073741824 | bytes 4194304 | tf_op jit(solution)/shard_map/pallas_call | solution.py:181
  152.3 6.9 %shard_map.80 = bf16[512,256]{1,0:T(8,128)(2,1)} custom-call(s32[10]{0:T(128)} %pad_add_fusion.info_ref, bf16[512,256]{1,0:T(8,128)(2,1)} %shard_map.79.q_ref, bf16[4096,256]{1,0:T(8,128)(2,1)} %constant_dynamic-update-slice_fusion.kv_ref, s32[512,1]{1,0:T(8,128)} %copy.12.qseg_ref, s32[8,1,512]{2,1,0:T(1,128)} %bitcast.55), custom_call_target="tpu_custom_call" | custom-call | flops 1073741824 | bytes 4194304 | tf_op jit(solution)/shard_map/pallas_call | solution.py:181
  159.1 6.8 %shard_map.78 = bf16[512,256]{1,0:T(8,128)(2,1)} custom-call(s32[10]{0:T(128)} %pad_add_fusion.info_ref, bf16[512,256]{1,0:T(8,128)(2,1)} %shard_map.77.q_ref, bf16[4096,256]{1,0:T(8,128)(2,1)} %constant_dynamic-update-slice_fusion.kv_ref, s32[512,1]{1,0:T(8,128)} %copy.12.qseg_ref, s32[8,1,512]{2,1,0:T(1,128)} %bitcast.56), custom_call_target="tpu_custom_call" | custom-call | flops 1073741824 | bytes 4194304 | tf_op jit(solution)/shard_map/pallas_call | solution.py:181
  166.1 7.2 %shard_map.76 = bf16[512,256]{1,0:T(8,128)(2,1)} custom-call(s32[10]{0:T(128)} %pad_add_fusion.info_ref, bf16[512,256]{1,0:T(8,128)(2,1)} %shard_map.74.q_ref, bf16[4096,256]{1,0:T(8,128)(2,1)} %constant_dynamic-update-slice_fusion.kv_ref, s32[512,1]{1,0:T(8,128)} %copy.12.qseg_ref, s32[8,1,512]{2,1,0:T(1,128)} %bitcast.57), custom_call_target="tpu_custom_call" | custom-call | flops 1073741824 | bytes 4194304 | tf_op jit(solution)/shard_map/pallas_call | solution.py:181
  173.5 8.1 %collective-permute-done.12 = bf16[512,256]{1,0:T(8,128)(2,1)S(1)} collective-permute-done((bf16[512,256]{1,0:T(8,128)(2,1)}, bf16[512,256]{1,0:T(8,128)(2,1)S(1)}, u32[]{:S(2)}, u32[]{:S(2)}) %collective-permute-start.12) | collective-permute-done | bytes 262176 | tf_op jit(solution)/shard_map/ppermute | solution.py:210
  181.8 14.3 %convolution_convert_fusion = bf16[1024,4096]{1,0:T(8,128)(2,1)} fusion(bf16[1024,4096]{1,0:T(8,128)(2,1)} %param.10, bf16[1024,256]{1,0:T(8,128)(2,1)S(1)} %bitcast.42, bf16[1024,256]{1,0:T(8,128)(2,1)S(1)} %bitcast.43, bf16[1024,256]{1,0:T(8,128)(2,1)S(1)} %bitcast.44, bf16[1024,256]{1,0:T(8,128)(2,1)S(1)} %bitcast.45), kind=kOutput, calls=%fused_computation | convolution fusion | flops 8602517504 | bytes 18874368 | tf_op jit(solution)/shard_map/dot_general | solution.py:283
  196.1 159.7 %reduce-scatter.2.cloned.1.call-done = bf16[256,4096]{1,0:T(8,128)(2,1)} async-done(((bf16[1024,4096]{1,0:T(8,128)(2,1)}), bf16[256,4096]{1,0:T(8,128)(2,1)}) %reduce-scatter.2.cloned.1.call-update) | async-done | bytes 2097168 | tf_op jit(solution)/shard_map/reduce_scatter | solution.py:284
  (109 shorter events, 14.3 us)
Async XLA Ops:
  6.5 349.3 %reduce-scatter.2.cloned.1.call-start = ((), (), s32[]{:S(2)}) async-start(), calls=%async_computation.1 | async-start | bytes 10485760 | tf_op jit(solution)/shard_map/reduce_scatter | solution.py:284
  6.5 43.2 %copy-start.20 = (s32[4]{0:T(128)S(1)}, s32[4]{0:T(128)}, u32[]{:S(2)}) copy-start(s32[4]{0:T(128)} %constant.72.clone) | copy-start | bytes 52
  6.5 43.2 %copy-start.18 = (s32[4096]{0:T(1024)S(1)}, s32[4096]{0:T(1024)}, u32[]{:S(2)}) copy-start(s32[4096]{0:T(1024)} %param.11) | copy-start | bytes 49156
  6.5 43.9 %copy-start.19 = (bf16[8192]{0:T(1024)(128)(2,1)S(1)}, bf16[8192]{0:T(1024)(128)(2,1)}, u32[]{:S(2)}) copy-start(bf16[8192]{0:T(1024)(128)(2,1)} %param.8) | copy-start | bytes 49156
  9.5 15.8 %collective-permute-start.4 = (bf16[1024,256]{1,0:T(8,128)(2,1)S(1)}, bf16[1024,256]{1,0:T(8,128)(2,1)}, u32[]{:S(2)}, u32[]{:S(2)}) collective-permute-start(bf16[1024,256]{1,0:T(8,128)(2,1)S(1)} %get-tuple-element.7), channel_id=1, source_target_pairs={{0,4},{4,0},{1,5},{5,1},{2,6},{6,2},{3,7},{7,3},{8,12},{12,8},{9,1... | collective-permute-start | bytes 1572872 | tf_op jit(solution)/shard_map/ppermute | solution.py:210
  12.5 24.0 %collective-permute-start.23 = (bf16[1024,256]{1,0:T(8,128)(2,1)S(1)}, bf16[1024,256]{1,0:T(8,128)(2,1)S(1)}, u32[]{:S(2)}, u32[]{:S(2)}) collective-permute-start(bf16[1024,256]{1,0:T(8,128)(2,1)S(1)} %get-tuple-element.8), channel_id=1, source_target_pairs={{0,4},{4,0},{1,5},{5,1},{2,6},{6,2},{3,7},{7,3},{8,12},{12,8},{9,1... | collective-permute-start | bytes 1572872 | tf_op jit(solution)/shard_map/ppermute | solution.py:210
  25.3 13.3 %collective-permute-start.5 = (bf16[1024,256]{1,0:T(8,128)(2,1)}, bf16[1024,256]{1,0:T(8,128)(2,1)}, u32[]{:S(2)}, u32[]{:S(2)}) collective-permute-start(bf16[1024,256]{1,0:T(8,128)(2,1)} %collective-permute-done.4.q0), channel_id=1, source_target_pairs={{0,16},{8,24},{16,0},{24,8},{1,17},{9,25},{17,1},{25,9},{2,18},{10... | collective-permute-start | bytes 1572872 | tf_op jit(solution)/shard_map/ppermute | solution.py:214
  27.3 20.3 %collective-permute-start.18 = (bf16[1024,256]{1,0:T(8,128)(2,1)S(1)}, bf16[1024,256]{1,0:T(8,128)(2,1)S(1)}, u32[]{:S(2)}, u32[]{:S(2)}) collective-permute-start(bf16[1024,256]{1,0:T(8,128)(2,1)S(1)} %get-tuple-element.9), channel_id=1, source_target_pairs={{0,4},{4,0},{1,5},{5,1},{2,6},{6,2},{3,7},{7,3},{8,12},{12,8},{9,1... | collective-permute-start | bytes 1572872 | tf_op jit(solution)/shard_map/ppermute | solution.py:210
  28.9 32.8 %collective-permute-start.13 = (bf16[1024,256]{1,0:T(8,128)(2,1)}, bf16[1024,256]{1,0:T(8,128)(2,1)S(1)}, u32[]{:S(2)}, u32[]{:S(2)}) collective-permute-start(bf16[1024,256]{1,0:T(8,128)(2,1)} %get-tuple-element.6), channel_id=1, source_target_pairs={{0,4},{4,0},{1,5},{5,1},{2,6},{6,2},{3,7},{7,3},{8,12},{12,8},{9,1... | collective-permute-start | bytes 1572872 | tf_op jit(solution)/shard_map/ppermute | solution.py:210
  36.4 25.3 %collective-permute-start.24 = (bf16[1024,256]{1,0:T(8,128)(2,1)S(1)}, bf16[1024,256]{1,0:T(8,128)(2,1)S(1)}, u32[]{:S(2)}, u32[]{:S(2)}) collective-permute-start(bf16[1024,256]{1,0:T(8,128)(2,1)S(1)} %collective-permute-done.23.q0), channel_id=1, source_target_pairs={{0,16},{8,24},{16,0},{24,8},{1,17},{9,25},{17,1},{25,9},{2,18},{10... | collective-permute-start | bytes 1572872 | tf_op jit(solution)/shard_map/ppermute | solution.py:214
  38.5 26.4 %collective-permute-start.6 = (bf16[1024,256]{1,0:T(8,128)(2,1)}, bf16[1024,256]{1,0:T(8,128)(2,1)}, u32[]{:S(2)}, u32[]{:S(2)}) collective-permute-start(bf16[1024,256]{1,0:T(8,128)(2,1)} %collective-permute-done.4.q0), channel_id=1, source_target_pairs={{0,8},{8,0},{16,24},{24,16},{1,9},{9,1},{17,25},{25,17},{2,10},{10... | collective-permute-start | bytes 1572872 | tf_op jit(solution)/shard_map/ppermute | solution.py:214
  38.6 26.5 %collective-permute-start.7 = (bf16[1024,256]{1,0:T(8,128)(2,1)}, bf16[1024,256]{1,0:T(8,128)(2,1)}, u32[]{:S(2)}, u32[]{:S(2)}) collective-permute-start(bf16[1024,256]{1,0:T(8,128)(2,1)} %collective-permute-done.5.q1), channel_id=1, source_target_pairs={{0,8},{8,0},{16,24},{24,16},{1,9},{9,1},{17,25},{25,17},{2,10},{10... | collective-permute-start | bytes 1572872 | tf_op jit(solution)/shard_map/ppermute | solution.py:214
  47.7 27.9 %collective-permute-start = (bf16[1024,256]{1,0:T(8,128)(2,1)}, bf16[1024,256]{1,0:T(8,128)(2,1)S(1)}, u32[]{:S(2)}, u32[]{:S(2)}) collective-permute-start(bf16[1024,256]{1,0:T(8,128)(2,1)} %get-tuple-element.5), channel_id=1, source_target_pairs={{0,4},{4,0},{1,5},{5,1},{2,6},{6,2},{3,7},{7,3},{8,12},{12,8},{9,1... | collective-permute-start | bytes 1572872 | tf_op jit(solution)/shard_map/ppermute | solution.py:210
  61.7 19.0 %collective-permute-start.25 = (bf16[1024,256]{1,0:T(8,128)(2,1)S(1)}, bf16[1024,256]{1,0:T(8,128)(2,1)}, u32[]{:S(2)}, u32[]{:S(2)}) collective-permute-start(bf16[1024,256]{1,0:T(8,128)(2,1)S(1)} %collective-permute-done.23.q0), channel_id=1, source_target_pairs={{0,8},{8,0},{16,24},{24,16},{1,9},{9,1},{17,25},{25,17},{2,10},{10... | collective-permute-start | bytes 1572872 | tf_op jit(solution)/shard_map/ppermute | solution.py:214
  61.8 20.4 %collective-permute-start.19 = (bf16[1024,256]{1,0:T(8,128)(2,1)S(1)}, bf16[1024,256]{1,0:T(8,128)(2,1)}, u32[]{:S(2)}, u32[]{:S(2)}) collective-permute-start(bf16[1024,256]{1,0:T(8,128)(2,1)S(1)} %collective-permute-done.18.q0), channel_id=1, source_target_pairs={{0,16},{8,24},{16,0},{24,8},{1,17},{9,25},{17,1},{25,9},{2,18},{10... | collective-permute-start | bytes 1572872 | tf_op jit(solution)/shard_map/ppermute | solution.py:214
  64.9 18.2 %collective-permute-start.20 = (bf16[1024,256]{1,0:T(8,128)(2,1)S(1)}, bf16[1024,256]{1,0:T(8,128)(2,1)S(1)}, u32[]{:S(2)}, u32[]{:S(2)}) collective-permute-start(bf16[1024,256]{1,0:T(8,128)(2,1)S(1)} %collective-permute-done.18.q0), channel_id=1, source_target_pairs={{0,8},{8,0},{16,24},{24,16},{1,9},{9,1},{17,25},{25,17},{2,10},{10... | collective-permute-start | bytes 1572872 | tf_op jit(solution)/shard_map/ppermute | solution.py:214
  65.1 18.1 %collective-permute-start.26 = (bf16[1024,256]{1,0:T(8,128)(2,1)S(1)}, bf16[1024,256]{1,0:T(8,128)(2,1)}, u32[]{:S(2)}, u32[]{:S(2)}) collective-permute-start(bf16[1024,256]{1,0:T(8,128)(2,1)S(1)} %collective-permute-done.24.q1), channel_id=1, source_target_pairs={{0,8},{8,0},{16,24},{24,16},{1,9},{9,1},{17,25},{25,17},{2,10},{10... | collective-permute-start | bytes 1572872 | tf_op jit(solution)/shard_map/ppermute | solution.py:214
  75.6 9.4 %collective-permute-start.8 = (bf16[512,256]{1,0:T(8,128)(2,1)}, bf16[512,256]{1,0:T(8,128)(2,1)S(1)}, u32[]{:S(2)}, u32[]{:S(2)}) collective-permute-start(bf16[512,256]{1,0:T(8,128)(2,1)} %shard_map.75), channel_id=1, source_target_pairs={{0,16},{8,24},{16,0},{24,8},{1,17},{9,25},{17,1},{25,9},{2,18},{10... | collective-permute-start | bytes 786440 | tf_op jit(solution)/shard_map/ppermute | solution.py:214
  80.7 16.3 %collective-permute-start.14 = (bf16[1024,256]{1,0:T(8,128)(2,1)S(1)}, bf16[1024,256]{1,0:T(8,128)(2,1)S(1)}, u32[]{:S(2)}, u32[]{:S(2)}) collective-permute-start(bf16[1024,256]{1,0:T(8,128)(2,1)S(1)} %collective-permute-done.13.q0), channel_id=1, source_target_pairs={{0,16},{8,24},{16,0},{24,8},{1,17},{9,25},{17,1},{25,9},{2,18},{10... | collective-permute-start | bytes 1572872 | tf_op jit(solution)/shard_map/ppermute | solution.py:214
  82.2 24.4 %collective-permute-start.1 = (bf16[1024,256]{1,0:T(8,128)(2,1)S(1)}, bf16[1024,256]{1,0:T(8,128)(2,1)S(1)}, u32[]{:S(2)}, u32[]{:S(2)}) collective-permute-start(bf16[1024,256]{1,0:T(8,128)(2,1)S(1)} %collective-permute-done.q0), channel_id=1, source_target_pairs={{0,16},{8,24},{16,0},{24,8},{1,17},{9,25},{17,1},{25,9},{2,18},{10... | collective-permute-start | bytes 1572872 | tf_op jit(solution)/shard_map/ppermute | solution.py:214
  83.1 24.3 %collective-permute-start.21 = (bf16[1024,256]{1,0:T(8,128)(2,1)}, bf16[1024,256]{1,0:T(8,128)(2,1)S(1)}, u32[]{:S(2)}, u32[]{:S(2)}) collective-permute-start(bf16[1024,256]{1,0:T(8,128)(2,1)} %collective-permute-done.19.q1), channel_id=1, source_target_pairs={{0,8},{8,0},{16,24},{24,16},{1,9},{9,1},{17,25},{25,17},{2,10},{10... | collective-permute-start | bytes 1572872 | tf_op jit(solution)/shard_map/ppermute | solution.py:214
  83.2 23.5 %collective-permute-start.9 = (bf16[512,256]{1,0:T(8,128)(2,1)}, bf16[512,256]{1,0:T(8,128)(2,1)S(1)}, u32[]{:S(2)}, u32[]{:S(2)}) collective-permute-start(bf16[512,256]{1,0:T(8,128)(2,1)} %shard_map.75), channel_id=1, source_target_pairs={{0,4},{4,0},{1,5},{5,1},{2,6},{6,2},{3,7},{7,3},{8,12},{12,8},{9,1... | collective-permute-start | bytes 786440 | tf_op jit(solution)/shard_map/ppermute | solution.py:210
  85.0 22.2 %collective-permute-start.10 = (bf16[512,256]{1,0:T(8,128)(2,1)S(1)}, bf16[512,256]{1,0:T(8,128)(2,1)S(1)}, u32[]{:S(2)}, u32[]{:S(2)}) collective-permute-start(bf16[512,256]{1,0:T(8,128)(2,1)S(1)} %collective-permute-done.8), channel_id=1, source_target_pairs={{0,4},{4,0},{1,5},{5,1},{2,6},{6,2},{3,7},{7,3},{8,12},{12,8},{9,1... | collective-permute-start | bytes 786440 | tf_op jit(solution)/shard_map/ppermute | solution.py:210
  97.1 21.7 %collective-permute-start.15 = (bf16[1024,256]{1,0:T(8,128)(2,1)S(1)}, bf16[1024,256]{1,0:T(8,128)(2,1)S(1)}, u32[]{:S(2)}, u32[]{:S(2)}) collective-permute-start(bf16[1024,256]{1,0:T(8,128)(2,1)S(1)} %collective-permute-done.13.q0), channel_id=1, source_target_pairs={{0,8},{8,0},{16,24},{24,16},{1,9},{9,1},{17,25},{25,17},{2,10},{10... | collective-permute-start | bytes 1572872 | tf_op jit(solution)/shard_map/ppermute | solution.py:214
  106.7 23.8 %collective-permute-start.2 = (bf16[1024,256]{1,0:T(8,128)(2,1)S(1)}, bf16[1024,256]{1,0:T(8,128)(2,1)S(1)}, u32[]{:S(2)}, u32[]{:S(2)}) collective-permute-start(bf16[1024,256]{1,0:T(8,128)(2,1)S(1)} %collective-permute-done.q0), channel_id=1, source_target_pairs={{0,8},{8,0},{16,24},{24,16},{1,9},{9,1},{17,25},{25,17},{2,10},{10... | collective-permute-start | bytes 1572872 | tf_op jit(solution)/shard_map/ppermute | solution.py:214
  106.7 12.0 %collective-permute-start.16 = (bf16[1024,256]{1,0:T(8,128)(2,1)S(1)}, bf16[1024,256]{1,0:T(8,128)(2,1)S(1)}, u32[]{:S(2)}, u32[]{:S(2)}) collective-permute-start(bf16[1024,256]{1,0:T(8,128)(2,1)S(1)} %collective-permute-done.14.q1), channel_id=1, source_target_pairs={{0,8},{8,0},{16,24},{24,16},{1,9},{9,1},{17,25},{25,17},{2,10},{10... | collective-permute-start | bytes 1572872 | tf_op jit(solution)/shard_map/ppermute | solution.py:214
  107.2 23.3 %collective-permute-start.3 = (bf16[1024,256]{1,0:T(8,128)(2,1)S(1)}, bf16[1024,256]{1,0:T(8,128)(2,1)S(1)}, u32[]{:S(2)}, u32[]{:S(2)}) collective-permute-start(bf16[1024,256]{1,0:T(8,128)(2,1)S(1)} %collective-permute-done.1.q1), channel_id=1, source_target_pairs={{0,8},{8,0},{16,24},{24,16},{1,9},{9,1},{17,25},{25,17},{2,10},{10... | collective-permute-start | bytes 1572872 | tf_op jit(solution)/shard_map/ppermute | solution.py:214
  107.4 37.0 %collective-permute-start.11 = (bf16[2048,256]{1,0:T(8,128)(2,1)S(1)}, bf16[2048,256]{1,0:T(8,128)(2,1)S(1)}, u32[]{:S(2)}, u32[]{:S(2)}) collective-permute-start(bf16[2048,256]{1,0:T(8,128)(2,1)S(1)} %pad_maximum_fusion), channel_id=1, source_target_pairs={{0,8},{8,0},{16,24},{24,16},{1,9},{9,1},{17,25},{25,17},{2,10},{10... | collective-permute-start | bytes 3145736 | tf_op jit(solution)/shard_map/ppermute | solution.py:214
  152.3 21.0 %collective-permute-start.27 = (bf16[512,256]{1,0:T(8,128)(2,1)}, bf16[512,256]{1,0:T(8,128)(2,1)S(1)}, u32[]{:S(2)}, u32[]{:S(2)}) collective-permute-start(bf16[512,256]{1,0:T(8,128)(2,1)} %shard_map.82), channel_id=1, source_target_pairs={{0,4},{4,0},{1,5},{5,1},{2,6},{6,2},{3,7},{7,3},{8,12},{12,8},{9,1... | collective-permute-start | bytes 786440 | tf_op jit(solution)/shard_map/ppermute | solution.py:210
  159.1 14.2 %collective-permute-start.22 = (bf16[512,256]{1,0:T(8,128)(2,1)}, bf16[512,256]{1,0:T(8,128)(2,1)S(1)}, u32[]{:S(2)}, u32[]{:S(2)}) collective-permute-start(bf16[512,256]{1,0:T(8,128)(2,1)} %shard_map.80), channel_id=1, source_target_pairs={{0,4},{4,0},{1,5},{5,1},{2,6},{6,2},{3,7},{7,3},{8,12},{12,8},{9,1... | collective-permute-start | bytes 786440 | tf_op jit(solution)/shard_map/ppermute | solution.py:210
  166.0 7.5 %collective-permute-start.17 = (bf16[512,256]{1,0:T(8,128)(2,1)}, bf16[512,256]{1,0:T(8,128)(2,1)S(1)}, u32[]{:S(2)}, u32[]{:S(2)}) collective-permute-start(bf16[512,256]{1,0:T(8,128)(2,1)} %shard_map.78), channel_id=1, source_target_pairs={{0,4},{4,0},{1,5},{5,1},{2,6},{6,2},{3,7},{7,3},{8,12},{12,8},{9,1... | collective-permute-start | bytes 786440 | tf_op jit(solution)/shard_map/ppermute | solution.py:210
  173.2 8.5 %collective-permute-start.12 = (bf16[512,256]{1,0:T(8,128)(2,1)}, bf16[512,256]{1,0:T(8,128)(2,1)S(1)}, u32[]{:S(2)}, u32[]{:S(2)}) collective-permute-start(bf16[512,256]{1,0:T(8,128)(2,1)} %shard_map.76), channel_id=1, source_target_pairs={{0,4},{4,0},{1,5},{5,1},{2,6},{6,2},{3,7},{7,3},{8,12},{12,8},{9,1... | collective-permute-start | bytes 786440 | tf_op jit(solution)/shard_map/ppermute | solution.py:210
  (19 other events, 248.8 us)
Sparse Core Ops, SparseCore 0:
  196.3 159.5 reduce-scatter.1

commit v2 on v0

--- a/solution.py
+++ b/solution.py
@@ -1,18 +1,23 @@
+import functools
 import math
 
 import jax
 import jax.numpy as jnp
 from jax import lax
+from jax.experimental import pallas as pl
+from jax.experimental.pallas import tpu as pltpu
 from jax.sharding import PartitionSpec as P
 
 QUERY_HEAD_COUNT = 32
 KV_HEAD_COUNT = 4
 HEAD_SIZE = 128
 BLOCK = 512
-
+GROUP_WIDTH = QUERY_HEAD_COUNT // KV_HEAD_COUNT
 
 THETA = 500000.0
 NEG_BIG = -1e30
+PARTS = 2
+OUT_PARTS = 4
 
 
 def rope_tables(positions):
@@ -29,6 +34,346 @@
     return (jnp.cos(angles), jnp.sin(angles))
 
 
+VMEM = pl.BlockSpec(memory_space=pltpu.VMEM)
+SMEM = pl.BlockSpec(memory_space=pltpu.SMEM)
+ANY = pl.BlockSpec(memory_space=pl.ANY)
+
+
+def call(kernel, specs, shapes, operands, flops, scratch=(), vmem=16):
+    return pl.pallas_call(
+        kernel,
+        in_specs=specs,
+        out_specs=[VMEM] * len(shapes),
+        out_shape=[jax.ShapeDtypeStruct(shape, dtype) for shape, dtype in shapes],
+        scratch_shapes=scratch,
+        compiler_params=pltpu.CompilerParams(vmem_limit_bytes=vmem * 1024 * 1024),
+        cost_estimate=pl.CostEstimate(flops=flops, bytes_accessed=0, transcendentals=0),
+    )(*operands)
+
+
+def norm_kernel(hidden_ref, gain_ref, out_ref):
+    tile = 64
+
+    def body(i, carry):
+        rows = pl.ds(pl.multiple_of(i * tile, tile), tile)
+        widened = hidden_ref[rows, :].astype(jnp.float32)
+        inverse_rms = lax.rsqrt(jnp.mean(widened * widened, axis=1, keepdims=True) + 1e-05)
+        out_ref[rows, :] = (widened * inverse_rms * gain_ref[...].astype(jnp.float32)).astype(
+            jnp.bfloat16
+        )
+        return carry
+
+    lax.fori_loop(0, hidden_ref.shape[0] // tile, body, 0)
+
+
+def norm_rows(hidden, gain):
+    rows, width = hidden.shape
+    return call(
+        norm_kernel,
+        [VMEM, VMEM],
+        [(hidden.shape, jnp.bfloat16)],
+        (hidden, gain.reshape(1, width)),
+        rows * width * 8,
+    )[0]
+
+
+def proj_kernel(first_column, rotated, count, start_ref, normed_ref, *refs):
+    pieces = refs[:count]
+    cos_ref, sin_ref, own_ref, out_ref, scratch, sems = refs[count:]
+    columns = out_ref.shape[1]
+    depth = own_ref.shape[0]
+    part = depth // 4
+    copies = [
+        pltpu.make_async_copy(
+            own_ref.at[pl.ds(i * part, part), pl.ds(first_column, columns)],
+            scratch.at[pl.ds(i * part, part)],
+            sems.at[i],
+        )
+        for i in range(4)
+    ]
+    for copy in copies:
+        copy.start()
+    total = None
+    for i, piece in enumerate(pieces):
+        features = pl.ds(pl.multiple_of(start_ref[1 + i], 512), piece.shape[0])
+        product = jnp.dot(normed_ref[:, features], piece[...], preferred_element_type=jnp.float32)
+        total = product if total is None else total + product
+    for copy in copies:
+        copy.wait()
+    features = pl.ds(pl.multiple_of(start_ref[0], 512), depth)
+    total += jnp.dot(normed_ref[:, features], scratch[...], preferred_element_type=jnp.float32)
+    for i in range(columns // HEAD_SIZE):
+        lanes = slice(i * HEAD_SIZE, (i + 1) * HEAD_SIZE)
+        head = total[:, lanes]
+        if i < rotated:
+            head = head * cos_ref[...] + pltpu.roll(head, HEAD_SIZE // 2, 1) * sin_ref[...]
+        out_ref[:, lanes] = head.astype(jnp.bfloat16)
+
+
+def project(starts, normed, own, pieces, first_column, rotated, cos_table, sin_table):
+    rows, width = normed.shape
+    columns = pieces[0].shape[1]
+    return call(
+        functools.partial(proj_kernel, first_column, rotated, len(pieces)),
+        [SMEM, VMEM, *[VMEM] * len(pieces), VMEM, VMEM, ANY],
+        [((rows, columns), jnp.bfloat16)],
+        (starts, normed, *pieces, cos_table, sin_table, own),
+        2 * rows * width * columns,
+        [pltpu.VMEM((own.shape[0], columns), jnp.bfloat16), pltpu.SemaphoreType.DMA((4,))],
+    )[0]
+
+
+def attend_kernel(count, info_ref, q_ref, first_ref, *refs):
+    near = refs[:count]
+    out_ref, m_ref, l_ref, acc_ref = refs[count:]
+    my_block = info_ref[0]
+    first_block = info_ref[1]
+    scale = math.log2(math.e) / math.sqrt(HEAD_SIZE)
+    rows = q_ref.shape[0]
+    heads = q_ref.shape[1] // HEAD_SIZE
+
+    def one_block(block, diagonal):
+        slot = info_ref[2 + block]
+        begin = pl.multiple_of((slot % (8 // count)) * BLOCK, BLOCK)
+        keys, values = [], []
+        pair = near[0][pl.ds(begin, BLOCK), :]
+        for i in range(1, count):
+            pair = jnp.where(slot // (8 // count) == i, near[i][pl.ds(begin, BLOCK), :], pair)
+        keys, values = pair[:, :HEAD_SIZE], pair[:, HEAD_SIZE:].T
+        place = lax.broadcasted_iota(jnp.int32, (BLOCK, rows), 0)
+        allowed = place >= first_ref[...] - block * BLOCK
+        if diagonal:
+            allowed &= place <= lax.broadcasted_iota(jnp.int32, (BLOCK, rows), 1)
+        for h in range(heads):
+            lanes = slice(h * HEAD_SIZE, (h + 1) * HEAD_SIZE)
+            scores = lax.dot_general(
+                keys, q_ref[:, lanes], (((1,), (1,)), ((), ())), preferred_element_type=jnp.float32
+            )
+            scores = jnp.where(allowed, scores, NEG_BIG)
+            new_max = jnp.max(scores, axis=0, keepdims=True)
+            if not diagonal:
+                old_max = m_ref[h]
+                new_max = jnp.maximum(old_max, new_max)
+            weights = jnp.exp2((scores - new_max) * scale)
+            block_sum = jnp.sum(weights, axis=0, keepdims=True)
+            product = jnp.dot(
+                values, weights.astype(jnp.bfloat16), preferred_element_type=jnp.float32
+            )
+            if diagonal:
+                l_ref[h] = block_sum
+                acc_ref[h] = product
+            else:
+                factor = jnp.exp2((old_max - new_max) * scale)
+                l_ref[h] = l_ref[h] * factor + block_sum
+                acc_ref[h] = acc_ref[h] * factor + product
+            m_ref[h] = new_max
+
+    one_block(my_block, True)
+
+    def body(i, carry):
+        one_block(my_block - i, False)
+        return carry
+
+    lax.fori_loop(1, my_block - first_block + 1, body, 0)
+    for h in range(heads):
+        lanes = slice(h * HEAD_SIZE, (h + 1) * HEAD_SIZE)
+        out_ref[:, lanes] = (acc_ref[h] / l_ref[h]).T.astype(jnp.bfloat16)
+
+
+def attend(info, queries, pairs, first_key):
+    rows, columns = queries.shape
+    heads = columns // HEAD_SIZE
+    return call(
+        functools.partial(attend_kernel, len(pairs)),
+        [SMEM, VMEM, VMEM, *[VMEM] * len(pairs)],
+        [(queries.shape, jnp.bfloat16)],
+        (info, queries, first_key, *pairs),
+        4 * rows * 4 * BLOCK * columns,
+        [
+            pltpu.VMEM((heads, 1, rows), jnp.float32),
+            pltpu.VMEM((heads, 1, rows), jnp.float32),
+            pltpu.VMEM((heads, HEAD_SIZE, rows), jnp.float32),
+        ],
+    )[0]
+
+
+def out_kernel(first_column, parts, info_ref, *refs):
+    mine, theirs, far = (refs[i * parts : (i + 1) * parts] for i in range(3))
+    quarters = refs[3 * parts : 3 * parts + 4]
+    own_ref, keep_ref, send_ref, own_weights, lhs, total, sem = refs[3 * parts + 4 :]
+    half, columns = keep_ref.shape
+    copy = pltpu.make_async_copy(own_ref.at[:, pl.ds(first_column, columns)], own_weights, sem)
+    copy.start()
+
+    def gather(pieces):
+        start = 0
+        for piece in pieces:
+            width = piece.shape[1]
+            lhs[:, start : start + width] = piece[...]
+            start += width
+
+    gather(far)
+    products = []
+    for i, quarter in enumerate(quarters):
+        depth = quarter.shape[0]
+        heads = pl.ds(pl.multiple_of(info_ref[2 + i], depth), depth)
+        products.append(
+            jnp.dot(lhs[:, heads], quarter[...], preferred_element_type=jnp.float32)
+        )
+    total[...] = sum(products[1:], products[0])
+
+    @pl.when(info_ref[0] == 1)
+    def _():
+        gather(mine)
+
+    @pl.when(info_ref[0] == 0)
+    def _():
+        gather(theirs)
+
+    copy.wait()
+    total[...] += jnp.dot(lhs[...], own_weights[...], preferred_element_type=jnp.float32)
+    keep_at = pl.multiple_of(info_ref[1], half)
+    keep_ref[...] = total[pl.ds(keep_at, half), :]
+    send_ref[...] = total[pl.ds(half - keep_at, half), :].astype(jnp.bfloat16)
+
+
+def project_out(info, mine, theirs, far, quarters, own, first_column):
+    rows = mine[0].shape[0]
+    depth, columns = own.shape[0], quarters[0].shape[1]
+    half = rows // 2
+    return call(
+        functools.partial(out_kernel, first_column, len(mine)),
+        [SMEM, *[VMEM] * (3 * len(mine) + 4), ANY],
+        [((half, columns), jnp.float32), ((half, columns), jnp.bfloat16)],
+        (info, *mine, *theirs, *far, *quarters, own),
+        4 * rows * depth * columns,
+        [
+            pltpu.VMEM((depth, columns), jnp.bfloat16),
+            pltpu.VMEM((rows, depth), jnp.bfloat16),
+            pltpu.VMEM((rows, columns), jnp.float32),
+            pltpu.SemaphoreType.DMA,
+        ],
+    )
+
+
+def swap_uly(array):
+    return lax.ppermute(array, "uly", [(0, 1), (1, 0)])
+
+
+def swap(array, name, bit):
+    return lax.ppermute(array, name, [(i, i ^ bit) for i in range(4)])
+
+
+def pick(table, index):
+    ids = jnp.arange(table.shape[0])
+    return jnp.sum(jnp.where(index[..., None] == ids, table, 0), axis=-1)
+
+
+def spread(first):
+    second = swap(first, "blk", 2)
+    return [first, second, swap(first, "blk", 1), swap(second, "blk", 1)]
+
+
+def one_block_each(hidden, norm_gain, query_key_value_weight, w_out, doc_ids, block_order):
+    blk, uly, tp = (lax.axis_index(name) for name in ("blk", "uly", "tp"))
+    weights = query_key_value_weight.reshape(query_key_value_weight.shape[0], -1)
+    depth = weights.shape[0] // 4
+    nblocks = block_order.shape[0]
+    peers = blk ^ jnp.array([0, 2, 1, 3])
+
+    query_width = GROUP_WIDTH * HEAD_SIZE
+    part = query_width // PARTS
+
+    def rows_of(start, size, first_column, columns):
+        return swap_uly(
+            lax.dynamic_slice(weights, (blk * depth + start, first_column), (size, columns))
+        )
+
+    pair_first = [rows_of(0, depth, query_width, 2 * HEAD_SIZE)]
+    query_first = [
+        [rows_of(h * depth // 2, depth // 2, p * part, part) for h in range(2)]
+        for p in range(PARTS)
+    ]
+
+    out_depth, out_width = w_out.shape
+    out_part = out_width // OUT_PARTS
+    out_first = [
+        swap(
+            lax.dynamic_slice(
+                w_out, (blk * (out_depth // 4), p * out_part), (out_depth // 4, out_part)
+            ),
+            "tp",
+            2,
+        )
+        for p in range(OUT_PARTS)
+    ]
+
+    normed = norm_rows(hidden, norm_gain)
+
+    my_row = blk * 2 + uly
+    my_block = pick(block_order, my_row)
+    positions = my_block * BLOCK + jnp.arange(BLOCK)
+    cosine, sine = rope_tables(positions)
+    cos_table = jnp.concatenate([cosine, cosine], axis=1)
+    sin_table = jnp.concatenate([-sine, sine], axis=1)
+    base = uly * weights.shape[0]
+    other = (1 - uly) * weights.shape[0] + peers * depth
+
+    rows_of_slots = jnp.stack(
+        [(blk ^ c ^ x) * 2 + (uly ^ u) for c in (0, 1) for u in (0, 1) for x in (0, 2)]
+    )
+    blocks_of_slots = pick(block_order, rows_of_slots)
+    slots = jnp.arange(nblocks)
+    slot_of_block = jnp.sum(
+        jnp.where(blocks_of_slots[None, :] == slots[:, None], slots[None, :], 0), axis=1
+    )
+    query_seg = lax.dynamic_slice(doc_ids, (my_block * BLOCK,), (BLOCK,))
+    first_key = jnp.sum((doc_ids[:, None] < query_seg[None, :]).astype(jnp.int32), axis=0)
+    info = jnp.concatenate([jnp.stack([my_block, first_key[0] // BLOCK]), slot_of_block])
+    first_key = first_key[None, :]
+
+    pair_starts = jnp.concatenate([base[None], other])
+    pair = project(
+        pair_starts,
+        normed,
+        weights,
+        spread(pair_first[0]),
+        query_width,
+        1,
+        cos_table,
+        sin_table,
+    )
+    query_pieces = [[spread(first) for first in firsts] for firsts in query_first]
+    pair_x = swap(pair, "blk", 2)
+    near = jnp.concatenate([pair, pair_x, swap_uly(pair), swap_uly(pair_x)], axis=0)
+    pairs = (near, swap(near, "blk", 1))
+
+    query_starts = jnp.concatenate([base[None], other, other + depth // 2])
+    mine, theirs, far = [], [], []
+    use_own = (uly == 0) == (tp < 2)
+    for p in range(PARTS):
+        pieces = query_pieces[p][0] + query_pieces[p][1]
+        queries = project(
+            query_starts, normed, weights, pieces, p * part, part // HEAD_SIZE, cos_table, sin_table
+        )
+        a = attend(info, queries, pairs, first_key)
+        b = swap_uly(a)
+        mine.append(a)
+        theirs.append(b)
+        far.append(swap(jnp.where(use_own, b, a), "tp", 2))
+
+    out_info = jnp.concatenate(
+        [jnp.stack([use_own.astype(jnp.int32), (tp % 2) * (BLOCK // 2)]), peers * (out_depth // 4)]
+    )
+    results = []
+    for p in range(OUT_PARTS):
+        keep, send = project_out(
+            out_info, mine, theirs, far, spread(out_first[p]), w_out, p * out_part
+        )
+        results.append((keep + swap(send, "tp", 1).astype(jnp.float32)).astype(jnp.bfloat16))
+    return jnp.concatenate(results, axis=1)
+
+
 def rotate(values, cos_table, sin_table):
     half_dim = values.shape[-1] // 2
     leading = values[..., :half_dim]
@@ -52,7 +397,7 @@
     head_dim = queries.shape[2]
     inv_root = 1.0 / math.sqrt(head_dim)
 
-    def attend(running, pieces, offset):
+    def attend_pieces(running, pieces):
         key_piece, value_piece = pieces
         key_count = key_piece.shape[0]
         block_size = key_count
@@ -95,11 +440,11 @@
         final_state, unused = lax.scan(one_block, running, stacked)
         return final_state
 
-    return attend
+    return attend_pieces
 
 
 def on_device(hidden, norm_gain, query_key_value_weight, w_out, doc_ids, block_order):
-    group_width = QUERY_HEAD_COUNT // KV_HEAD_COUNT
+    group_width = GROUP_WIDTH
     heads_here = group_width // lax.axis_size("uly")
     widened = hidden.astype(jnp.float32)
     inverse_rms = lax.rsqrt(jnp.mean(widened * widened, axis=1, keepdims=True) + 1e-05)
@@ -133,21 +478,19 @@
         jnp.bfloat16
     )
     values_local = pair_sum[:, HEAD_SIZE:].astype(jnp.bfloat16)
-    attend = make_attend(queries, query_pos, query_seg, doc_ids, block_order)
+    attend_pieces = make_attend(queries, query_pos, query_seg, doc_ids, block_order)
     initial = (
         jnp.full((heads_here, block_len), NEG_BIG, jnp.float32),
         jnp.zeros((heads_here, block_len), jnp.float32),
         jnp.zeros((heads_here, block_len, HEAD_SIZE), jnp.float32),
     )
-    final_state = attend(
+    row_max, row_sum, weighted = attend_pieces(
         initial,
         (
             lax.all_gather(keys_local, ("blk", "uly"), axis=0, tiled=True),
             lax.all_gather(values_local, ("blk", "uly"), axis=0, tiled=True),
         ),
-        jnp.int32(0),
-    )
-    row_max, row_sum, weighted = final_state
+    )
     attended = (weighted / row_sum[:, :, None]).astype(jnp.bfloat16)
     head_weights = w_out.reshape(group_width, HEAD_SIZE, w_out.shape[1])
     projected_rows = jnp.einsum(
@@ -162,10 +505,17 @@
 
 
 def solution(mesh):
-    return jax.shard_map(
-        on_device,
-        mesh=mesh,
-        in_specs=(P(("blk", "uly"), None), P(), P("uly", "tp", None), P("tp", "uly"), P(), P()),
-        out_specs=P(("blk", "tp"), "uly"),
-        check_vma=False,
-    )
+    sizes = dict(mesh.shape)
+
+    def whole(hidden, *rest):
+        tokens = hidden.shape[0]
+        fits = (sizes["blk"], sizes["uly"], sizes["tp"]) == (4, 2, 4) and tokens == 8 * BLOCK
+        return jax.shard_map(
+            one_block_each if fits else on_device,
+            mesh=mesh,
+            in_specs=(P(("blk", "uly"), None), P(), P("uly", "tp", None), P("tp", "uly"), P(), P()),
+            out_specs=P(("blk", "tp"), "uly"),
+            check_vma=False,
+        )(hidden, *rest)
+
+    return whole

time: 598 us -> 324 us (0.54)
  blocking collectives: 98.1 us -> 0 us
  matrix products: 87.6 us -> 0 us
  waiting for transfers between devices: 261 us -> 183 us
  Pallas kernels: 0 us -> 60.3 us
  local copies, waits for them, and re-layouts: 81.2 us -> 27.3 us
  other arithmetic: 53.9 us -> 8.73 us
  starting transfers between devices: 0.39 us -> 37.6 us
  between operations: 13.8 us -> 3.8 us
    reduce_scatter x3 -> x0, waiting for transfers between devices: 220 us -> none  [the longest x1 145 us: on_device(): lax.psum_scatter(projected_rows.astype(jnp.bfloat16), 'tp', scatter_dimen...]
    ppermute x0 -> x48, waiting for transfers between devices: none -> 183 us  [the longest x39 153 us: swap(): return lax.ppermute(array, name, [(i, i ^ bit) for i in range(4)])]
    all_to_all x1 -> x0, blocking collectives: 98.1 us -> none  [on_device(): lax.all_to_all(rms_scaled, 'uly', split_axis=1, concat_axis=0, tiled=True)]
    dot_general x10 -> x0, matrix products: 87.6 us -> none  [the longest x4 30.2 us: one_block(): jnp.einsum('hqk,kd->hqd', weights.astype(jnp.bfloat16), value_blk, prefer...]
    pallas_call x0 -> x10, Pallas kernels: none -> 60.3 us  [call(): pl.pallas_call(kernel, in_specs=specs, out_specs=[VMEM] * len(shapes), ou...]
    all_gather x3 -> x0, waiting for transfers between devices: 41.4 us -> none  [the longest x1 33.2 us: on_device(): lax.all_gather(attended, 'uly', axis=0, tiled=True)]
    ppermute x0 -> x48, starting transfers between devices: none -> 37.6 us  [the longest x39 27.5 us: swap(): return lax.ppermute(array, name, [(i, i ^ bit) for i in range(4)])]
    reduce_sum x8 -> x4, other arithmetic: 38.5 us -> 1.91 us  [the longest x1 0.97 us: one_block_each(): jnp.sum((doc_ids[:, None] < query_seg[None, :]).astype(jnp.int32), axis=0)]
  transfers between devices with their start and end apart: 6 -> 48, of which waited for: 5 -> 19; matrix products, arithmetic and copies ran while one was open for 7% -> 4% of each run, Pallas kernels for 0% -> 19%
where the time goes in v2:
time: 324 us; the launch traced here: 321 us
  waiting for transfers between devices  183 us (56%)
  Pallas kernels  60.3 us (19%)
  starting transfers between devices  37.6 us (12%)
  local copies, waits for them, and re-layouts  27.3 us (8%)
  other arithmetic  8.73 us (3%)
  between operations  3.8 us (1%)
    ppermute x39, waiting for transfers between devices, swap(): return lax.ppermute(array, name, [(i, i ^ bit) for i in range(4)])  153 us
    pallas_call x10, Pallas kernels, call(): pl.pallas_call(kernel, in_specs=specs, out_specs=[VMEM] * len(shapes), ou...  60.3 us
    ppermute x9, waiting for transfers between devices, swap_uly(): return lax.ppermute(array, 'uly', [(0, 1), (1, 0)])  30.5 us
    ppermute x39, starting transfers between devices, swap(): return lax.ppermute(array, name, [(i, i ^ bit) for i in range(4)])  27.5 us
    unnamed x56, local copies, waits for them, and re-layouts  20 us
    ppermute x9, starting transfers between devices, swap_uly(): return lax.ppermute(array, 'uly', [(0, 1), (1, 0)])  10.1 us
  transfers between devices with their start and end apart: 48, of which 19 were waited for; matrix products, arithmetic and copies ran while one was open for 4% of the time, Pallas kernels for 19%

profile of v2, /device:TPU:0, one launch (start us, length us, event | category | flops | bytes accessed | tf_op | source)
XLA Modules:
  0.0 321.0 jit_solution(16572130131721934512)
XLA Ops:
  4.1 11.9 %collective-permute-done.8.refs_0_ = bf16[1024,256]{1,0:T(8,128)(2,1)S(1)} collective-permute-done((bf16[1024,256]{1,0:T(8,128)(2,1)S(1)}, bf16[1024,256]{1,0:T(8,128)(2,1)S(1)}, u32[]{:S(2)}, u32[]{:S(2)}) %collective-permute-start.8) | collective-permute-done | bytes 524320 | tf_op jit(solution)/shard_map/ppermute | solution.py:260
  25.5 3.7 %collective-permute-done.9.refs_1_ = bf16[1024,256]{1,0:T(8,128)(2,1)} collective-permute-done((bf16[1024,256]{1,0:T(8,128)(2,1)S(1)}, bf16[1024,256]{1,0:T(8,128)(2,1)}, u32[]{:S(2)}, u32[]{:S(2)}) %collective-permute-start.9) | collective-permute-done | bytes 524320 | tf_op jit(solution)/shard_map/ppermute | solution.py:264
  31.2 3.4 %copy-done.5 = bf16[512,8192]{1,0:T(8,128)(2,1)S(1)} copy-done((bf16[512,8192]{1,0:T(8,128)(2,1)S(1)}, bf16[512,8192]{1,0:T(8,128)(2,1)}, u32[]{:S(2)}) %copy-start.5) | copy-done | bytes 8388632
  34.6 5.2 %shard_map.73.normed_ref = bf16[512,8192]{1,0:T(8,128)(2,1)S(1)} custom-call(bf16[512,8192]{1,0:T(8,128)(2,1)S(1)} %copy-done.5, bf16[1,8192]{1,0:T(2,128)(2,1)S(1)} %reshape.43.gain_ref), custom_call_target="tpu_custom_call" | custom-call | flops 33554432 | tf_op jit(solution)/shard_map/pallas_call | solution.py:43
  40.2 7.5 %shard_map.75 = bf16[512,256]{1,0:T(8,128)(2,1)S(1)} custom-call(s32[5]{0:T(128)S(1)} %pad_add_fusion.3.start_ref, bf16[512,8192]{1,0:T(8,128)(2,1)S(1)} %shard_map.73.normed_ref, bf16[1024,256]{1,0:T(8,128)(2,1)S(1)} %collective-permute-done.8.refs_0_, bf16[1024,256]{1,0:T(8,128)(2,1)} %collective-permute-done.9.refs_1_, ...), custom_call_target="tpu_custom_call" | custom-call | flops 2147483648 | tf_op jit(solution)/shard_map/pallas_call | solution.py:43
  51.2 5.3 %collective-permute-done.12 = bf16[512,256]{1,0:T(8,128)(2,1)S(1)} collective-permute-done((bf16[512,256]{1,0:T(8,128)(2,1)S(1)}, bf16[512,256]{1,0:T(8,128)(2,1)S(1)}, u32[]{:S(2)}, u32[]{:S(2)}) %collective-permute-start.12) | collective-permute-done | bytes 262176 | tf_op jit(solution)/shard_map/ppermute | solution.py:264
  59.4 15.6 %collective-permute-done.13 = bf16[512,256]{1,0:T(8,128)(2,1)S(1)} collective-permute-done((bf16[512,256]{1,0:T(8,128)(2,1)S(1)}, bf16[512,256]{1,0:T(8,128)(2,1)S(1)}, u32[]{:S(2)}, u32[]{:S(2)}) %collective-permute-start.13) | collective-permute-done | bytes 262176 | tf_op jit(solution)/shard_map/ppermute | solution.py:260
  82.2 3.9 %collective-permute-done.5.refs_5_ = bf16[512,512]{1,0:T(8,128)(2,1)} collective-permute-done((bf16[512,512]{1,0:T(8,128)(2,1)}, bf16[512,512]{1,0:T(8,128)(2,1)}, u32[]{:S(2)}, u32[]{:S(2)}) %collective-permute-start.5) | collective-permute-done | bytes 524320 | tf_op jit(solution)/shard_map/ppermute | solution.py:264
  93.6 3.7 %collective-permute-done.17.refs_1_ = bf16[512,512]{1,0:T(8,128)(2,1)} collective-permute-done((bf16[512,512]{1,0:T(8,128)(2,1)}, bf16[512,512]{1,0:T(8,128)(2,1)}, u32[]{:S(2)}, u32[]{:S(2)}) %collective-permute-start.17) | collective-permute-done | bytes 524320 | tf_op jit(solution)/shard_map/ppermute | solution.py:264
  99.9 7.2 %collective-permute-done.21.refs_5_ = bf16[512,512]{1,0:T(8,128)(2,1)} collective-permute-done((bf16[512,512]{1,0:T(8,128)(2,1)S(1)}, bf16[512,512]{1,0:T(8,128)(2,1)}, u32[]{:S(2)}, u32[]{:S(2)}) %collective-permute-start.21) | collective-permute-done | bytes 524320 | tf_op jit(solution)/shard_map/ppermute | solution.py:264
  108.1 3.4 %copy-done.2 = bf16[512,8192]{1,0:T(8,128)(2,1)S(1)} copy-done((bf16[512,8192]{1,0:T(8,128)(2,1)S(1)}, bf16[512,8192]{1,0:T(8,128)(2,1)}, u32[]{:S(2)}) %copy-start.2) | copy-done | bytes 8388632
  111.5 4.0 %copy-done.3 = bf16[4096,1,1280]{2,0,1:T(8,128)(2,1)S(1)} copy-done((bf16[4096,1,1280]{2,0,1:T(8,128)(2,1)S(1)}, bf16[4096,1,1280]{2,0,1:T(8,128)(2,1)}, u32[]{:S(2)}) %copy-start.3) | copy-done | bytes 10485784
  116.5 7.1 %shard_map.74.q_ref = bf16[512,512]{1,0:T(8,128)(2,1)S(1)} custom-call(s32[9]{0:T(128)S(1)} %pad_add_fusion.2.start_ref, bf16[512,8192]{1,0:T(8,128)(2,1)S(1)} %copy-done.2, bf16[512,512]{1,0:T(8,128)(2,1)} %collective-permute-done.refs_0_, bf16[512,512]{1,0:T(8,128)(2,1)S(1)} %collective-permute-done.1.refs_1_, bf16[512,512]{1,0:T(8,128)(2,1)S(1)} %copy-done.17, ...), custom_call_target="tpu_custom_call" | custom-call | flops 4294967296 | tf_op jit(solution)/shard_map/pallas_call | solution.py:43
  123.6 8.4 %shard_map.76.refs_0_ = bf16[512,512]{1,0:T(8,128)(2,1)S(1)} custom-call(s32[10]{0:T(128)S(1)} %pad_add_fusion.1.info_ref, bf16[512,512]{1,0:T(8,128)(2,1)S(1)} %shard_map.74.q_ref, s32[1,512]{1,0:T(1,128)S(1)} %bitcast.31, bf16[2048,256]{1,0:T(8,128)(2,1)S(1)} %pad_maximum_fusion.1.refs_0_, bf16[2048,256]{1,0:T(8,128)(2,1)} %collective-permute-done.15.refs_1_), custom_call_target="tpu_custom_call" | custom-call | flops 2147483648 | tf_op jit(solution)/shard_map/pallas_call | solution.py:43
  137.7 6.5 %shard_map.77.q_ref = bf16[512,512]{1,0:T(8,128)(2,1)S(1)} custom-call(s32[9]{0:T(128)S(1)} %pad_add_fusion.2.start_ref, bf16[512,8192]{1,0:T(8,128)(2,1)S(1)} %copy-done.2, bf16[512,512]{1,0:T(8,128)(2,1)} %collective-permute-done.16.refs_0_, bf16[512,512]{1,0:T(8,128)(2,1)} %collective-permute-done.17.refs_1_, ...), custom_call_target="tpu_custom_call" | custom-call | flops 4294967296 | tf_op jit(solution)/shard_map/pallas_call | solution.py:43
  144.2 8.2 %shard_map.78.refs_1_ = bf16[512,512]{1,0:T(8,128)(2,1)S(1)} custom-call(s32[10]{0:T(128)S(1)} %pad_add_fusion.1.info_ref, bf16[512,512]{1,0:T(8,128)(2,1)S(1)} %shard_map.77.q_ref, s32[1,512]{1,0:T(1,128)S(1)} %bitcast.32, bf16[2048,256]{1,0:T(8,128)(2,1)S(1)} %copy-done.7, bf16[2048,256]{1,0:T(8,128)(2,1)} %collective-permute-done.15.refs_1_), custom_call_target="tpu_custom_call" | custom-call | flops 2147483648 | tf_op jit(solution)/shard_map/pallas_call | solution.py:43
  152.5 26.9 %collective-permute-done.38.refs_6_ = bf16[256,1024]{1,0:T(8,128)(2,1)} collective-permute-done((bf16[256,1024]{1,0:T(8,128)(2,1)S(1)}, bf16[256,1024]{1,0:T(8,128)(2,1)}, u32[]{:S(2)}, u32[]{:S(2)}) %collective-permute-start.38) | collective-permute-done | bytes 524320 | tf_op jit(solution)/shard_map/ppermute | solution.py:264
  179.4 11.2 %collective-permute-done.33.refs_6_ = bf16[256,1024]{1,0:T(8,128)(2,1)} collective-permute-done((bf16[256,1024]{1,0:T(8,128)(2,1)S(1)}, bf16[256,1024]{1,0:T(8,128)(2,1)}, u32[]{:S(2)}, u32[]{:S(2)}) %collective-permute-start.33) | collective-permute-done | bytes 524320 | tf_op jit(solution)/shard_map/ppermute | solution.py:264
  190.7 10.1 %collective-permute-done.28.refs_6_ = bf16[256,1024]{1,0:T(8,128)(2,1)} collective-permute-done((bf16[256,1024]{1,0:T(8,128)(2,1)}, bf16[256,1024]{1,0:T(8,128)(2,1)}, u32[]{:S(2)}, u32[]{:S(2)}) %collective-permute-start.28) | collective-permute-done | bytes 524320 | tf_op jit(solution)/shard_map/ppermute | solution.py:264
  204.8 11.1 %collective-permute-done.39.refs_7_ = bf16[256,1024]{1,0:T(8,128)(2,1)} collective-permute-done((bf16[256,1024]{1,0:T(8,128)(2,1)}, bf16[256,1024]{1,0:T(8,128)(2,1)}, u32[]{:S(2)}, u32[]{:S(2)}) %collective-permute-start.39) | collective-permute-done | bytes 524320 | tf_op jit(solution)/shard_map/ppermute | solution.py:264
  219.6 7.5 %collective-permute-done.34.refs_7_ = bf16[256,1024]{1,0:T(8,128)(2,1)} collective-permute-done((bf16[256,1024]{1,0:T(8,128)(2,1)}, bf16[256,1024]{1,0:T(8,128)(2,1)}, u32[]{:S(2)}, u32[]{:S(2)}) %collective-permute-start.34) | collective-permute-done | bytes 524320 | tf_op jit(solution)/shard_map/ppermute | solution.py:264
  227.1 9.1 %collective-permute-done.29.refs_7_ = bf16[256,1024]{1,0:T(8,128)(2,1)} collective-permute-done((bf16[256,1024]{1,0:T(8,128)(2,1)}, bf16[256,1024]{1,0:T(8,128)(2,1)}, u32[]{:S(2)}, u32[]{:S(2)}) %collective-permute-start.29) | collective-permute-done | bytes 524320 | tf_op jit(solution)/shard_map/ppermute | solution.py:264
  237.6 14.8 %collective-permute-done.26.refs_4_ = bf16[512,512]{1,0:T(8,128)(2,1)S(1)} collective-permute-done((bf16[512,512]{1,0:T(8,128)(2,1)}, bf16[512,512]{1,0:T(8,128)(2,1)S(1)}, u32[]{:S(2)}, u32[]{:S(2)}) %collective-permute-start.26) | collective-permute-done | bytes 524320 | tf_op jit(solution)/shard_map/ppermute | solution.py:264
  252.5 8.0 %collective-permute-done.27.refs_5_ = bf16[512,512]{1,0:T(8,128)(2,1)S(1)} collective-permute-done((bf16[512,512]{1,0:T(8,128)(2,1)}, bf16[512,512]{1,0:T(8,128)(2,1)S(1)}, u32[]{:S(2)}, u32[]{:S(2)}) %collective-permute-start.27) | collective-permute-done | bytes 524320 | tf_op jit(solution)/shard_map/ppermute | solution.py:264
  260.5 3.4 %copy-done = bf16[1024,4096]{1,0:T(8,128)(2,1)S(1)} copy-done((bf16[1024,4096]{1,0:T(8,128)(2,1)S(1)}, bf16[1024,4096]{1,0:T(8,128)(2,1)}, u32[]{:S(2)}) %copy-start) | copy-done | bytes 8388632
  267.0 4.3 %shard_map.82 = (f32[256,1024]{1,0:T(8,128)S(1)}, bf16[256,1024]{1,0:T(8,128)(2,1)S(1)}) custom-call(s32[6]{0:T(128)S(1)} %pad_add_fusion.info_ref, bf16[512,512]{1,0:T(8,128)(2,1)S(1)} %shard_map.76.refs_0_, bf16[512,512]{1,0:T(8,128)(2,1)S(1)} %shard_map.78.refs_1_, bf16[512,512]{1,0:T(8,128)(2,1)S(1)} %collective-permute-done.24.refs_2_, ...), custom_call_target="tpu_custom_call" | custom-call | flops 2147483648 | tf_op jit(solution)/shard_map/pallas_call | solution.py:43
  271.4 4.4 %shard_map.81 = (f32[256,1024]{1,0:T(8,128)S(1)}, bf16[256,1024]{1,0:T(8,128)(2,1)S(1)}) custom-call(s32[6]{0:T(128)S(1)} %pad_add_fusion.info_ref, bf16[512,512]{1,0:T(8,128)(2,1)S(1)} %shard_map.76.refs_0_, bf16[512,512]{1,0:T(8,128)(2,1)S(1)} %shard_map.78.refs_1_, bf16[512,512]{1,0:T(8,128)(2,1)S(1)} %collective-permute-done.24.refs_2_, ...), custom_call_target="tpu_custom_call" | custom-call | flops 2147483648 | tf_op jit(solution)/shard_map/pallas_call | solution.py:43
  277.8 4.5 %shard_map.80 = (f32[256,1024]{1,0:T(8,128)S(1)}, bf16[256,1024]{1,0:T(8,128)(2,1)S(1)}) custom-call(s32[6]{0:T(128)S(1)} %pad_add_fusion.info_ref, bf16[512,512]{1,0:T(8,128)(2,1)S(1)} %shard_map.76.refs_0_, bf16[512,512]{1,0:T(8,128)(2,1)S(1)} %shard_map.78.refs_1_, bf16[512,512]{1,0:T(8,128)(2,1)S(1)} %collective-permute-done.24.refs_2_, ...), custom_call_target="tpu_custom_call" | custom-call | flops 2147483648 | tf_op jit(solution)/shard_map/pallas_call | solution.py:43
  282.4 4.2 %shard_map.79 = (f32[256,1024]{1,0:T(8,128)S(1)}, bf16[256,1024]{1,0:T(8,128)(2,1)S(1)}) custom-call(s32[6]{0:T(128)S(1)} %pad_add_fusion.info_ref, bf16[512,512]{1,0:T(8,128)(2,1)S(1)} %shard_map.76.refs_0_, bf16[512,512]{1,0:T(8,128)(2,1)S(1)} %shard_map.78.refs_1_, bf16[512,512]{1,0:T(8,128)(2,1)S(1)} %collective-permute-done.24.refs_2_, ...), custom_call_target="tpu_custom_call" | custom-call | flops 2147483648 | tf_op jit(solution)/shard_map/pallas_call | solution.py:43
  288.8 8.5 %collective-permute-done.42 = bf16[256,1024]{1,0:T(8,128)(2,1)S(1)} collective-permute-done((bf16[256,1024]{1,0:T(8,128)(2,1)S(1)}, bf16[256,1024]{1,0:T(8,128)(2,1)S(1)}, u32[]{:S(2)}, u32[]{:S(2)}) %collective-permute-start.42) | collective-permute-done | bytes 524320 | tf_op jit(solution)/shard_map/ppermute | solution.py:264
  297.5 11.1 %collective-permute-done.37 = bf16[256,1024]{1,0:T(8,128)(2,1)S(1)} collective-permute-done((bf16[256,1024]{1,0:T(8,128)(2,1)S(1)}, bf16[256,1024]{1,0:T(8,128)(2,1)S(1)}, u32[]{:S(2)}, u32[]{:S(2)}) %collective-permute-start.37) | collective-permute-done | bytes 524320 | tf_op jit(solution)/shard_map/ppermute | solution.py:264
  308.7 10.7 %collective-permute-done.32 = bf16[256,1024]{1,0:T(8,128)(2,1)S(1)} collective-permute-done((bf16[256,1024]{1,0:T(8,128)(2,1)S(1)}, bf16[256,1024]{1,0:T(8,128)(2,1)S(1)}, u32[]{:S(2)}, u32[]{:S(2)}) %collective-permute-start.32) | collective-permute-done | bytes 524320 | tf_op jit(solution)/shard_map/ppermute | solution.py:264
  (159 shorter events, 62.5 us)
Async XLA Ops:
  20.7 30.1 %collective-permute-start = (bf16[512,512]{1,0:T(8,128)(2,1)}, bf16[512,512]{1,0:T(8,128)(2,1)}, u32[]{:S(2)}, u32[]{:S(2)}) collective-permute-start(bf16[512,512]{1,0:T(8,128)(2,1)} %get-tuple-element.25), channel_id=1, source_target_pairs={{0,4},{4,0},{1,5},{5,1},{2,6},{6,2},{3,7},{7,3},{8,12},{12,8},{9,1... | collective-permute-start | bytes 1572872 | tf_op jit(solution)/shard_map/ppermute | solution.py:260
  22.2 35.7 %collective-permute-start.4 = (bf16[512,512]{1,0:T(8,128)(2,1)}, bf16[512,512]{1,0:T(8,128)(2,1)}, u32[]{:S(2)}, u32[]{:S(2)}) collective-permute-start(bf16[512,512]{1,0:T(8,128)(2,1)} %get-tuple-element.24), channel_id=1, source_target_pairs={{0,4},{4,0},{1,5},{5,1},{2,6},{6,2},{3,7},{7,3},{8,12},{12,8},{9,1... | collective-permute-start | bytes 1572872 | tf_op jit(solution)/shard_map/ppermute | solution.py:260
  22.7 36.7 %collective-permute-start.16 = (bf16[512,512]{1,0:T(8,128)(2,1)}, bf16[512,512]{1,0:T(8,128)(2,1)}, u32[]{:S(2)}, u32[]{:S(2)}) collective-permute-start(bf16[512,512]{1,0:T(8,128)(2,1)} %get-tuple-element.26), channel_id=1, source_target_pairs={{0,4},{4,0},{1,5},{5,1},{2,6},{6,2},{3,7},{7,3},{8,12},{12,8},{9,1... | collective-permute-start | bytes 1572872 | tf_op jit(solution)/shard_map/ppermute | solution.py:260
  49.2 29.2 %collective-permute-start.20 = (bf16[512,512]{1,0:T(8,128)(2,1)S(1)}, bf16[512,512]{1,0:T(8,128)(2,1)S(1)}, u32[]{:S(2)}, u32[]{:S(2)}) collective-permute-start(bf16[512,512]{1,0:T(8,128)(2,1)S(1)} %copy-done.20), channel_id=1, source_target_pairs={{0,4},{4,0},{1,5},{5,1},{2,6},{6,2},{3,7},{7,3},{8,12},{12,8},{9,1... | collective-permute-start | bytes 1572872 | tf_op jit(solution)/shard_map/ppermute | solution.py:260
  50.7 24.3 %collective-permute-start.13 = (bf16[512,256]{1,0:T(8,128)(2,1)S(1)}, bf16[512,256]{1,0:T(8,128)(2,1)S(1)}, u32[]{:S(2)}, u32[]{:S(2)}) collective-permute-start(bf16[512,256]{1,0:T(8,128)(2,1)S(1)} %shard_map.75), channel_id=1, source_target_pairs={{0,4},{4,0},{1,5},{5,1},{2,6},{6,2},{3,7},{7,3},{8,12},{12,8},{9,1... | collective-permute-start | bytes 786440 | tf_op jit(solution)/shard_map/ppermute | solution.py:260
  56.5 21.8 %collective-permute-start.14 = (bf16[512,256]{1,0:T(8,128)(2,1)S(1)}, bf16[512,256]{1,0:T(8,128)(2,1)S(1)}, u32[]{:S(2)}, u32[]{:S(2)}) collective-permute-start(bf16[512,256]{1,0:T(8,128)(2,1)S(1)} %collective-permute-done.12), channel_id=1, source_target_pairs={{0,4},{4,0},{1,5},{5,1},{2,6},{6,2},{3,7},{7,3},{8,12},{12,8},{9,1... | collective-permute-start | bytes 786440 | tf_op jit(solution)/shard_map/ppermute | solution.py:260
  57.9 22.1 %collective-permute-start.1 = (bf16[512,512]{1,0:T(8,128)(2,1)}, bf16[512,512]{1,0:T(8,128)(2,1)S(1)}, u32[]{:S(2)}, u32[]{:S(2)}) collective-permute-start(bf16[512,512]{1,0:T(8,128)(2,1)} %collective-permute-done.refs_0_), channel_id=1, source_target_pairs={{0,16},{8,24},{16,0},{24,8},{1,17},{9,25},{17,1},{25,9},{2,18},{10... | collective-permute-start | bytes 1572872 | tf_op jit(solution)/shard_map/ppermute | solution.py:264
  78.4 29.3 %collective-permute-start.15 = (bf16[2048,256]{1,0:T(8,128)(2,1)S(1)}, bf16[2048,256]{1,0:T(8,128)(2,1)}, u32[]{:S(2)}, u32[]{:S(2)}) collective-permute-start(bf16[2048,256]{1,0:T(8,128)(2,1)S(1)} %pad_maximum_fusion.1.refs_0_), channel_id=1, source_target_pairs={{0,8},{8,0},{16,24},{24,16},{1,9},{9,1},{17,25},{25,17},{2,10},{10... | collective-permute-start | bytes 3145736 | tf_op jit(solution)/shard_map/ppermute | solution.py:264
  80.8 26.3 %collective-permute-start.21 = (bf16[512,512]{1,0:T(8,128)(2,1)S(1)}, bf16[512,512]{1,0:T(8,128)(2,1)}, u32[]{:S(2)}, u32[]{:S(2)}) collective-permute-start(bf16[512,512]{1,0:T(8,128)(2,1)S(1)} %collective-permute-done.20.refs_4_), channel_id=1, source_target_pairs={{0,16},{8,24},{16,0},{24,8},{1,17},{9,25},{17,1},{25,9},{2,18},{10... | collective-permute-start | bytes 1572872 | tf_op jit(solution)/shard_map/ppermute | solution.py:264
  97.3 34.7 %collective-permute-start.43 = (bf16[256,1024]{1,0:T(8,128)(2,1)S(1)}, bf16[256,1024]{1,0:T(8,128)(2,1)S(1)}, u32[]{:S(2)}, u32[]{:S(2)}) collective-permute-start(bf16[256,1024]{1,0:T(8,128)(2,1)S(1)} %get-tuple-element.30), channel_id=1, source_target_pairs={{0,2},{1,3},{2,0},{3,1},{4,6},{5,7},{6,4},{7,5},{8,10},{9,11},{10,... | collective-permute-start | bytes 1572872 | tf_op jit(solution)/shard_map/ppermute | solution.py:264
  107.1 27.6 %collective-permute-start.18 = (bf16[512,512]{1,0:T(8,128)(2,1)}, bf16[512,512]{1,0:T(8,128)(2,1)S(1)}, u32[]{:S(2)}, u32[]{:S(2)}) collective-permute-start(bf16[512,512]{1,0:T(8,128)(2,1)} %collective-permute-done.16.refs_0_), channel_id=1, source_target_pairs={{0,8},{8,0},{16,24},{24,16},{1,9},{9,1},{17,25},{25,17},{2,10},{10... | collective-permute-start | bytes 1572872 | tf_op jit(solution)/shard_map/ppermute | solution.py:264
  107.1 28.0 %collective-permute-start.22 = (bf16[512,512]{1,0:T(8,128)(2,1)S(1)}, bf16[512,512]{1,0:T(8,128)(2,1)S(1)}, u32[]{:S(2)}, u32[]{:S(2)}) collective-permute-start(bf16[512,512]{1,0:T(8,128)(2,1)S(1)} %collective-permute-done.20.refs_4_), channel_id=1, source_target_pairs={{0,8},{8,0},{16,24},{24,16},{1,9},{9,1},{17,25},{25,17},{2,10},{10... | collective-permute-start | bytes 1572872 | tf_op jit(solution)/shard_map/ppermute | solution.py:264
  107.6 30.0 %collective-permute-start.19 = (bf16[512,512]{1,0:T(8,128)(2,1)}, bf16[512,512]{1,0:T(8,128)(2,1)S(1)}, u32[]{:S(2)}, u32[]{:S(2)}) collective-permute-start(bf16[512,512]{1,0:T(8,128)(2,1)} %collective-permute-done.17.refs_1_), channel_id=1, source_target_pairs={{0,8},{8,0},{16,24},{24,16},{1,9},{9,1},{17,25},{25,17},{2,10},{10... | collective-permute-start | bytes 1572872 | tf_op jit(solution)/shard_map/ppermute | solution.py:264
  107.7 30.0 %collective-permute-start.23 = (bf16[512,512]{1,0:T(8,128)(2,1)}, bf16[512,512]{1,0:T(8,128)(2,1)S(1)}, u32[]{:S(2)}, u32[]{:S(2)}) collective-permute-start(bf16[512,512]{1,0:T(8,128)(2,1)} %collective-permute-done.21.refs_5_), channel_id=1, source_target_pairs={{0,8},{8,0},{16,24},{24,16},{1,9},{9,1},{17,25},{25,17},{2,10},{10... | collective-permute-start | bytes 1572872 | tf_op jit(solution)/shard_map/ppermute | solution.py:264
  132.1 47.4 %collective-permute-start.38 = (bf16[256,1024]{1,0:T(8,128)(2,1)S(1)}, bf16[256,1024]{1,0:T(8,128)(2,1)}, u32[]{:S(2)}, u32[]{:S(2)}) collective-permute-start(bf16[256,1024]{1,0:T(8,128)(2,1)S(1)} %get-tuple-element.28), channel_id=1, source_target_pairs={{0,2},{1,3},{2,0},{3,1},{4,6},{5,7},{6,4},{7,5},{8,10},{9,11},{10,... | collective-permute-start | bytes 1572872 | tf_op jit(solution)/shard_map/ppermute | solution.py:264
  134.7 56.0 %collective-permute-start.33 = (bf16[256,1024]{1,0:T(8,128)(2,1)S(1)}, bf16[256,1024]{1,0:T(8,128)(2,1)}, u32[]{:S(2)}, u32[]{:S(2)}) collective-permute-start(bf16[256,1024]{1,0:T(8,128)(2,1)S(1)} %get-tuple-element.29), channel_id=1, source_target_pairs={{0,2},{1,3},{2,0},{3,1},{4,6},{5,7},{6,4},{7,5},{8,10},{9,11},{10,... | collective-permute-start | bytes 1572872 | tf_op jit(solution)/shard_map/ppermute | solution.py:264
  135.1 65.7 %collective-permute-start.28 = (bf16[256,1024]{1,0:T(8,128)(2,1)}, bf16[256,1024]{1,0:T(8,128)(2,1)}, u32[]{:S(2)}, u32[]{:S(2)}) collective-permute-start(bf16[256,1024]{1,0:T(8,128)(2,1)} %get-tuple-element.27), channel_id=1, source_target_pairs={{0,2},{1,3},{2,0},{3,1},{4,6},{5,7},{6,4},{7,5},{8,10},{9,11},{10,... | collective-permute-start | bytes 1572872 | tf_op jit(solution)/shard_map/ppermute | solution.py:264
  137.6 63.1 %collective-permute-start.44 = (bf16[256,1024]{1,0:T(8,128)(2,1)S(1)}, bf16[256,1024]{1,0:T(8,128)(2,1)}, u32[]{:S(2)}, u32[]{:S(2)}) collective-permute-start(bf16[256,1024]{1,0:T(8,128)(2,1)S(1)} %collective-permute-done.43.refs_6_), channel_id=1, source_target_pairs={{0,16},{8,24},{16,0},{24,8},{1,17},{9,25},{17,1},{25,9},{2,18},{10... | collective-permute-start | bytes 1572872 | tf_op jit(solution)/shard_map/ppermute | solution.py:264
  137.6 63.1 %collective-permute-start.24 = (bf16[512,512]{1,0:T(8,128)(2,1)S(1)}, bf16[512,512]{1,0:T(8,128)(2,1)S(1)}, u32[]{:S(2)}, u32[]{:S(2)}) collective-permute-start(bf16[512,512]{1,0:T(8,128)(2,1)S(1)} %shard_map.76.refs_0_), channel_id=1, source_target_pairs={{0,4},{4,0},{1,5},{5,1},{2,6},{6,2},{3,7},{7,3},{8,12},{12,8},{9,1... | collective-permute-start | bytes 1572872 | tf_op jit(solution)/shard_map/ppermute | solution.py:260
  179.4 24.3 %collective-permute-start.45 = (bf16[256,1024]{1,0:T(8,128)(2,1)S(1)}, bf16[256,1024]{1,0:T(8,128)(2,1)S(1)}, u32[]{:S(2)}, u32[]{:S(2)}) collective-permute-start(bf16[256,1024]{1,0:T(8,128)(2,1)S(1)} %collective-permute-done.43.refs_6_), channel_id=1, source_target_pairs={{0,8},{8,0},{16,24},{24,16},{1,9},{9,1},{17,25},{25,17},{2,10},{10... | collective-permute-start | bytes 1572872 | tf_op jit(solution)/shard_map/ppermute | solution.py:264
  200.7 26.4 %collective-permute-start.34 = (bf16[256,1024]{1,0:T(8,128)(2,1)}, bf16[256,1024]{1,0:T(8,128)(2,1)}, u32[]{:S(2)}, u32[]{:S(2)}) collective-permute-start(bf16[256,1024]{1,0:T(8,128)(2,1)} %collective-permute-done.33.refs_6_), channel_id=1, source_target_pairs={{0,16},{8,24},{16,0},{24,8},{1,17},{9,25},{17,1},{25,9},{2,18},{10... | collective-permute-start | bytes 1572872 | tf_op jit(solution)/shard_map/ppermute | solution.py:264
  203.7 32.6 %collective-permute-start.29 = (bf16[256,1024]{1,0:T(8,128)(2,1)}, bf16[256,1024]{1,0:T(8,128)(2,1)}, u32[]{:S(2)}, u32[]{:S(2)}) collective-permute-start(bf16[256,1024]{1,0:T(8,128)(2,1)} %collective-permute-done.28.refs_6_), channel_id=1, source_target_pairs={{0,16},{8,24},{16,0},{24,8},{1,17},{9,25},{17,1},{25,9},{2,18},{10... | collective-permute-start | bytes 1572872 | tf_op jit(solution)/shard_map/ppermute | solution.py:264
  203.7 32.6 %collective-permute-start.46 = (bf16[256,1024]{1,0:T(8,128)(2,1)}, bf16[256,1024]{1,0:T(8,128)(2,1)S(1)}, u32[]{:S(2)}, u32[]{:S(2)}) collective-permute-start(bf16[256,1024]{1,0:T(8,128)(2,1)} %collective-permute-done.44.refs_7_), channel_id=1, source_target_pairs={{0,8},{8,0},{16,24},{24,16},{1,9},{9,1},{17,25},{25,17},{2,10},{10... | collective-permute-start | bytes 1572872 | tf_op jit(solution)/shard_map/ppermute | solution.py:264
  215.9 36.6 %collective-permute-start.26 = (bf16[512,512]{1,0:T(8,128)(2,1)}, bf16[512,512]{1,0:T(8,128)(2,1)S(1)}, u32[]{:S(2)}, u32[]{:S(2)}) collective-permute-start(bf16[512,512]{1,0:T(8,128)(2,1)} %broadcast_select_fusion.1), channel_id=1, source_target_pairs={{0,2},{1,3},{2,0},{3,1},{4,6},{5,7},{6,4},{7,5},{8,10},{9,11},{10,... | collective-permute-start | bytes 1572872 | tf_op jit(solution)/shard_map/ppermute | solution.py:264
  216.7 43.8 %collective-permute-start.27 = (bf16[512,512]{1,0:T(8,128)(2,1)}, bf16[512,512]{1,0:T(8,128)(2,1)S(1)}, u32[]{:S(2)}, u32[]{:S(2)}) collective-permute-start(bf16[512,512]{1,0:T(8,128)(2,1)} %broadcast_select_fusion), channel_id=1, source_target_pairs={{0,2},{1,3},{2,0},{3,1},{4,6},{5,7},{6,4},{7,5},{8,10},{9,11},{10,... | collective-permute-start | bytes 1572872 | tf_op jit(solution)/shard_map/ppermute | solution.py:264
  227.1 44.2 %collective-permute-start.41 = (bf16[256,1024]{1,0:T(8,128)(2,1)}, bf16[256,1024]{1,0:T(8,128)(2,1)}, u32[]{:S(2)}, u32[]{:S(2)}) collective-permute-start(bf16[256,1024]{1,0:T(8,128)(2,1)} %collective-permute-done.39.refs_7_), channel_id=1, source_target_pairs={{0,8},{8,0},{16,24},{24,16},{1,9},{9,1},{17,25},{25,17},{2,10},{10... | collective-permute-start | bytes 1572872 | tf_op jit(solution)/shard_map/ppermute | solution.py:264
  236.3 39.5 %collective-permute-start.35 = (bf16[256,1024]{1,0:T(8,128)(2,1)}, bf16[256,1024]{1,0:T(8,128)(2,1)}, u32[]{:S(2)}, u32[]{:S(2)}) collective-permute-start(bf16[256,1024]{1,0:T(8,128)(2,1)} %collective-permute-done.33.refs_6_), channel_id=1, source_target_pairs={{0,8},{8,0},{16,24},{24,16},{1,9},{9,1},{17,25},{25,17},{2,10},{10... | collective-permute-start | bytes 1572872 | tf_op jit(solution)/shard_map/ppermute | solution.py:264
  237.1 40.8 %collective-permute-start.36 = (bf16[256,1024]{1,0:T(8,128)(2,1)}, bf16[256,1024]{1,0:T(8,128)(2,1)}, u32[]{:S(2)}, u32[]{:S(2)}) collective-permute-start(bf16[256,1024]{1,0:T(8,128)(2,1)} %collective-permute-done.34.refs_7_), channel_id=1, source_target_pairs={{0,8},{8,0},{16,24},{24,16},{1,9},{9,1},{17,25},{25,17},{2,10},{10... | collective-permute-start | bytes 1572872 | tf_op jit(solution)/shard_map/ppermute | solution.py:264
  252.5 30.0 %collective-permute-start.30 = (bf16[256,1024]{1,0:T(8,128)(2,1)}, bf16[256,1024]{1,0:T(8,128)(2,1)S(1)}, u32[]{:S(2)}, u32[]{:S(2)}) collective-permute-start(bf16[256,1024]{1,0:T(8,128)(2,1)} %collective-permute-done.28.refs_6_), channel_id=1, source_target_pairs={{0,8},{8,0},{16,24},{24,16},{1,9},{9,1},{17,25},{25,17},{2,10},{10... | collective-permute-start | bytes 1572872 | tf_op jit(solution)/shard_map/ppermute | solution.py:264
  260.5 22.0 %collective-permute-start.31 = (bf16[256,1024]{1,0:T(8,128)(2,1)}, bf16[256,1024]{1,0:T(8,128)(2,1)S(1)}, u32[]{:S(2)}, u32[]{:S(2)}) collective-permute-start(bf16[256,1024]{1,0:T(8,128)(2,1)} %collective-permute-done.29.refs_7_), channel_id=1, source_target_pairs={{0,8},{8,0},{16,24},{24,16},{1,9},{9,1},{17,25},{25,17},{2,10},{10... | collective-permute-start | bytes 1572872 | tf_op jit(solution)/shard_map/ppermute | solution.py:264
  282.3 26.2 %collective-permute-start.37 = (bf16[256,1024]{1,0:T(8,128)(2,1)S(1)}, bf16[256,1024]{1,0:T(8,128)(2,1)S(1)}, u32[]{:S(2)}, u32[]{:S(2)}) collective-permute-start(bf16[256,1024]{1,0:T(8,128)(2,1)S(1)} %get-tuple-element.16), channel_id=1, source_target_pairs={{0,1},{1,0},{2,3},{3,2},{4,5},{5,4},{6,7},{7,6},{8,9},{9,8},{10,11... | collective-permute-start | bytes 1572872 | tf_op jit(solution)/shard_map/ppermute | solution.py:264
  286.6 32.8 %collective-permute-start.32 = (bf16[256,1024]{1,0:T(8,128)(2,1)S(1)}, bf16[256,1024]{1,0:T(8,128)(2,1)S(1)}, u32[]{:S(2)}, u32[]{:S(2)}) collective-permute-start(bf16[256,1024]{1,0:T(8,128)(2,1)S(1)} %get-tuple-element.14), channel_id=1, source_target_pairs={{0,1},{1,0},{2,3},{3,2},{4,5},{5,4},{6,7},{7,6},{8,9},{9,8},{10,11... | collective-permute-start | bytes 1572872 | tf_op jit(solution)/shard_map/ppermute | solution.py:264
  (44 other events, 558.9 us)
